TPU v7x, 256 devices: a whole 4x4x8 slice. The times are simulated.
256 devices in a mesh: blk: 32 (over z_lo, x, core), users: 8 (over y, z_hi).
Axes of the slice: x: 4, y: 4, z: 8 (z_hi: 2, z_lo: 4; z = z_hi * 4 + z_lo), core: 2. Of those that a mesh axis runs over, the one named last changes fastest.
Arguments:
- interactions: bfloat16 [8192, 8192], P('users', 'blk'), may hold values from -0.125 to 0.125
- tile_mask: int32 [64, 64], P('users', 'blk'), may hold values from 0 to 1
- panel_of: int32 [32], replicated, may hold values from 0 to 31, each once
Outputs:
- gram: float32 [8192, 8192], P('users', 'blk')
All inputs are finite; a program needn't handle non-finite values.
Results may differ from a plain program's by a relative error of at most 0.0003.
Values may be sent and summed in bfloat16 or wider, within the bound.
No kernel may reach another device: no remote copies, remote signals or barrier semaphores. Data moves between devices by JAX's collectives and lax.ppermute only.
A program may use at most 128 MiB of HBM per device.

v0:
```python
import jax
import jax.numpy as jnp
from jax import lax
from jax.sharding import PartitionSpec as P

TILE = 128


def on_device(interactions, tile_mask, panel_of):
    user_rows = interactions.shape[0]
    width = interactions.shape[1]
    user_tiles = user_rows // TILE
    panel_tiles = width // TILE
    mask_values = tile_mask.astype(interactions.dtype)
    masked = (
        interactions.reshape(user_tiles, TILE, panel_tiles, TILE) * mask_values[:, None, :, None]
    ).reshape(user_rows, width)
    panels = panel_of.shape[0]
    item_count = width * panels
    contract = (((0,), (0,)), ((), ()))
    empty = jnp.zeros((item_count, width), jnp.float32)
    piece = lax.all_gather(masked, "blk", axis=1, tiled=True)
    product = lax.dot_general(piece, masked, contract, preferred_element_type=jnp.float32)
    stored_count = piece.shape[1] // width

    def put_panel(index, total):
        rows_block = lax.dynamic_slice_in_dim(product, index * width, width, 0)
        target = panel_of[index] * width
        return lax.dynamic_update_slice_in_dim(total, rows_block, target, 0)

    partial_rows = lax.fori_loop(0, stored_count, put_panel, empty)
    gram = lax.psum_scatter(partial_rows, "users", scatter_dimension=0, tiled=True)
    return gram


def solution(mesh):
    return jax.shard_map(
        on_device,
        mesh=mesh,
        in_specs=(P("users", "blk"), P("users", "blk"), P()),
        out_specs=P("users", "blk"),
        check_vma=False,
    )
```

profile of v0, /device:TPU:1, one launch (start us, length us, event | category | flops | bytes accessed | tf_op | source)
XLA Modules:
  0.0 439.8 jit_solution(12083452944130465425)
XLA Ops:
  7.7 1.9 bitcast_multiply_fusion
  9.6 127.7 %all-gather.2.cloned.1.call-done = bf16[1024,8192]{1,0:T(8,128)(2,1)} async-done(((bf16[1024,256]{1,0:T(8,128)(2,1)}), bf16[1024,8192]{1,0:T(8,128)(2,1)}) %all-gather.2.cloned.1.call-update) | async-done | bytes 16777232 | tf_op jit(solution)/shard_map/all_gather | solution.py:22
  137.3 13.8 %fusion = f32[8192,256]{1,0:T(8,128)} fusion(bf16[1024,8192]{1,0:T(8,128)(2,1)} %all-gather.2.cloned.1.call-done, bf16[1024,256]{1,0:T(8,128)(2,1)} %bitcast_multiply_fusion), kind=kOutput, calls=%fused_computation.2 | convolution fusion | flops 4294967296 | bytes 25690112 | tf_op jit(solution)/shard_map/dot_general | solution.py:23
  151.1 3.8 broadcast_in_dim.4
  154.9 93.5 %while.13 = (s32[]{:T(128)}, f32[8192,256]{1,0:T(8,128)}, f32[8192,256]{1,0:T(8,128)}, s32[32]{0:T(128)S(1)}, s32[]{:T(128)}, /*index=5*/s32[1]{0:T(128)}, s32[]{:T(128)}, s32[]{:T(128)}, s32[]{:T(128)}) while((s32[]{:T(128)}, f32[8192,256]{1,0:T(8,128)}, f32[8192,256]{1,0:T(8,128)}, s32[32]{0:T(128)S(1)}, s32[]{:T(128)}, ...), condition=%wide.region_1.0_spmd, body=%wide.region_0.0_spmd.sunk | while | flops 10 | bytes 524493 | solution.py:31
  156.1 1.7 dynamic-slice_dynamic-update-slice_fusion.2
  164.9 1.7 dynamic-slice_dynamic-update-slice_fusion.2
  167.8 1.7 dynamic-slice_dynamic-update-slice_fusion.2
  170.7 1.7 dynamic-slice_dynamic-update-slice_fusion.2
  179.5 1.7 dynamic-slice_dynamic-update-slice_fusion.2
  182.4 1.7 dynamic-slice_dynamic-update-slice_fusion.2
  191.1 1.7 dynamic-slice_dynamic-update-slice_fusion.2
  199.9 1.7 dynamic-slice_dynamic-update-slice_fusion.2
  202.9 1.7 dynamic-slice_dynamic-update-slice_fusion.2
  205.8 1.7 dynamic-slice_dynamic-update-slice_fusion.2
  208.7 1.7 dynamic-slice_dynamic-update-slice_fusion.2
  211.6 1.7 dynamic-slice_dynamic-update-slice_fusion.2
  226.2 1.7 dynamic-slice_dynamic-update-slice_fusion.2
  229.1 1.7 dynamic-slice_dynamic-update-slice_fusion.2
  235.0 1.7 dynamic-slice_dynamic-update-slice_fusion.2
  237.9 1.7 dynamic-slice_dynamic-update-slice_fusion.2
  240.8 1.7 dynamic-slice_dynamic-update-slice_fusion.2
  243.8 1.7 dynamic-slice_dynamic-update-slice_fusion.2
  248.4 184.5 %reduce-scatter.2.cloned.1.call-done = f32[1024,256]{1,0:T(8,128)} async-done(((f32[8192,256]{1,0:T(8,128)}), f32[1024,256]{1,0:T(8,128)}) %reduce-scatter.2.cloned.1.call-update) | async-done | bytes 1048592 | tf_op jit(solution)/shard_map/reduce_scatter | solution.py:32
  (55 shorter events, 43.1 us)
Async XLA Ops:
  6.5 130.8 %all-gather.2.cloned.1.call-start = ((), (), s32[]{:S(2)}) async-start(), calls=%async_computation.1 | async-start | bytes 17301504 | tf_op jit(solution)/shard_map/all_gather | solution.py:22
  9.6 423.3 %reduce-scatter.2.cloned.1.call-start = ((), (), s32[]{:S(2)}) async-start(), calls=%async_computation.2 | async-start | bytes 9437184 | tf_op jit(solution)/shard_map/reduce_scatter | solution.py:32
  151.1 3.8 copy-start
Sparse Core Ops, SparseCore 0:
  9.7 127.5 all-gather.1
  248.5 184.3 reduce-scatter.1
where the time goes:
time: 441 us; the launch traced here: 440 us
  waiting for transfers between devices  312 us (71%)
  local copies, waits for them, and re-layouts  76.4 us (17%)
  loops' own time  21.3 us (5%)
  matrix products  13.8 us (3%)
  between operations  13.4 us (3%)
    reduce_scatter x1, waiting for transfers between devices, on_device(): lax.psum_scatter(partial_rows, 'users', scatter_dimension=0, tiled=True)  185 us
    all_gather x1, waiting for transfers between devices, on_device(): piece = lax.all_gather(masked, 'blk', axis=1, tiled=True)  128 us
    dynamic_update_slice x32, local copies, waits for them, and re-layouts, put_panel(): return lax.dynamic_update_slice_in_dim(total, rows_block, target, 0)  53.6 us
    another operation x1, loops' own time, on_device(): partial_rows = lax.fori_loop(0, stored_count, put_panel, empty)  21.3 us
    dynamic_slice x32, local copies, waits for them, and re-layouts, put_panel(): target = panel_of[index] * width  18.6 us
    dot_general x1, matrix products, on_device(): lax.dot_general(piece, masked, contract, preferred_element_type=jnp.float32)  13.8 us
  transfers between devices with their start and end apart: 2, of which 2 were waited for; matrix products, arithmetic and copies ran while one was open for 0% of the time, Pallas kernels for 0%

commit v1 on v0

v1 whole, which is shorter than its diff:
```python
import jax
import jax.numpy as jnp
from jax import lax
from jax.sharding import PartitionSpec as P

TILE = 128
NZ, NX, NC = 4, 4, 2
NY, NH = 4, 2


def blk_pairs(dz=0, dx=0, flip=False):
    pairs = []
    for z in range(NZ):
        for x in range(NX):
            for c in range(NC):
                source = (((z + dz) % NZ) * NX + (x + dx) % NX) * NC + ((1 - c) if flip else c)
                pairs.append((source, (z * NX + x) * NC + c))
    return pairs


def user_pairs(dy=0, flip=False):
    pairs = []
    for y in range(NY):
        for h in range(NH):
            pairs.append((((y + dy) % NY) * NH + ((1 - h) if flip else h), y * NH + h))
    return pairs


def dot_rows(a, b):
    return lax.dot_general(a, b, (((0,), (0,)), ((), ())), preferred_element_type=jnp.float32)


def on_device(interactions, tile_mask, panel_of):
    rows, width = interactions.shape
    panels = panel_of.shape[0]
    mask = jnp.repeat(jnp.repeat(tile_mask.astype(interactions.dtype), TILE, 0), TILE, 1)
    masked = interactions * mask
    b = lax.axis_index("blk")
    u = lax.axis_index("users")
    core = b % NC
    place = b // NC
    y, h = u // NH, u % NH
    n_users = NY * NH
    piece = rows // panels
    places = panels // NC

    halves = masked.reshape(places, NC, piece, width)
    mine = lax.dynamic_index_in_dim(halves, core, 1, keepdims=False)
    other = lax.dynamic_index_in_dim(halves, 1 - core, 1, keepdims=False)
    got = lax.ppermute(other, "blk", blk_pairs(flip=True))
    pair = jnp.where(core == 0, jnp.concatenate([mine, got], -1), jnp.concatenate([got, mine], -1))
    across = lax.ppermute(pair, "users", user_pairs(flip=True))

    spread = lax.all_to_all(masked.reshape(panels, piece, width), "blk", 0, 0, tiled=True)
    inverse = jnp.zeros((panels,), jnp.int32).at[panel_of].set(jnp.arange(panels, dtype=jnp.int32))
    chosen = jnp.take(spread, inverse, axis=0)
    per_user = panels // n_users
    chosen = chosen.reshape(n_users, per_user, piece, width).transpose(0, 2, 1, 3)
    unit = lax.all_to_all(chosen.reshape(n_users, piece, per_user * width), "users", 0, 0, tiled=True)
    unit = unit.reshape(n_users * piece, per_user * width)
    half = unit.shape[0] // 2

    both = jnp.stack([jnp.where(h == 0, pair, across), jnp.where(h == 0, across, pair)], 0)
    up = lax.ppermute(both, "users", user_pairs(dy=1))
    down = lax.ppermute(both, "users", user_pairs(dy=-1))
    far_a = lax.ppermute(up[0], "users", user_pairs(dy=1))
    far_b = lax.ppermute(down[1], "users", user_pairs(dy=-1))
    far = jnp.stack([far_a, far_b], 0)
    cols = jnp.zeros((NY,) + both.shape, both.dtype)
    for dy, part in ((0, both), (1, up), (2, far), (3, down)):
        cols = lax.dynamic_update_slice_in_dim(cols, part[None], (y + dy) % NY, 0)
    cols = cols.reshape(n_users, places, piece, NC * width)

    zl, x = place // NX, place % NX
    total = None

    def add(total, a, dz, dx, lo, hi):
        at = ((zl + dz) % NZ) * NX + (x + dx) % NX
        part = lax.dynamic_index_in_dim(cols, at, 1, keepdims=False)
        part = part.reshape(n_users * piece, NC * width)[lo:hi]
        r = dot_rows(a, part)
        return r if total is None else total + r

    for dz in (0, 1, 3, 2):
        own = unit if dz == 0 else lax.ppermute(unit, "blk", blk_pairs(dz=dz))
        right = lax.ppermute(own, "blk", blk_pairs(dx=1))
        left = lax.ppermute(own, "blk", blk_pairs(dx=-1))
        far_r = lax.ppermute(right[:half], "blk", blk_pairs(dx=1))
        far_l = lax.ppermute(left[half:], "blk", blk_pairs(dx=-1))
        total = add(total, own, dz, 0, 0, 2 * half)
        total = add(total, right, dz, 1, 0, 2 * half)
        total = add(total, left, dz, 3, 0, 2 * half)
        total = add(total, far_r, dz, 2, 0, half)
        total = add(total, far_l, dz, 2, half, 2 * half)
    keep = lax.dynamic_slice_in_dim(total, core * width, width, 1)
    give = lax.dynamic_slice_in_dim(total, (1 - core) * width, width, 1)
    return keep + lax.ppermute(give, "blk", blk_pairs(flip=True))


def solution(mesh):
    return jax.shard_map(
        on_device,
        mesh=mesh,
        in_specs=(P("users", "blk"), P("users", "blk"), P()),
        out_specs=P("users", "blk"),
        check_vma=False,
    )
```

time: 441 us -> 209 us (0.47)
  the two profiles are of different devices: /device:TPU:1 before, /device:TPU:71 now
where the time goes in v1:
time: 209 us; the launch traced here: 208 us
  waiting for transfers between devices  83 us (40%)
  starting transfers between devices  55.7 us (27%)
  matrix products  39 us (19%)
  local copies, waits for them, and re-layouts  19.6 us (9%)
  other arithmetic  10.9 us (5%)
    dot_general x20, matrix products, dot_rows(): lax.dot_general(a, b, (((0,), (0,)), ((), ())), preferred_element_type=jn...  39 us
    ppermute x4, waiting for transfers between devices, on_device(): right = lax.ppermute(own, 'blk', blk_pairs(dx=1))  23.5 us
    ppermute x3, waiting for transfers between devices, on_device(): own = unit if dz == 0 else lax.ppermute(unit, 'blk', blk_pairs(dz=dz))  22.4 us
    ppermute x1, waiting for transfers between devices, on_device(): across = lax.ppermute(pair, 'users', user_pairs(flip=True))  18.2 us
    ppermute x4, starting transfers between devices, on_device(): left = lax.ppermute(own, 'blk', blk_pairs(dx=-1))  12.9 us
    all_to_all x1, starting transfers between devices, on_device(): lax.all_to_all(masked.reshape(panels, piece, width), 'blk', 0, 0, tiled=T...  7.56 us
    ppermute x4, starting transfers between devices, on_device(): far_l = lax.ppermute(left[half:], 'blk', blk_pairs(dx=-1))  6.82 us
    ppermute x1, waiting for transfers between devices, on_device(): up = lax.ppermute(both, 'users', user_pairs(dy=1))  6.27 us
  transfers between devices with their start and end apart: 28, of which 12 were waited for; matrix products, arithmetic and copies ran while one was open for 22% of the time, Pallas kernels for 0%

profile of v1, /device:TPU:71, one launch (start us, length us, event | category | flops | bytes accessed | tf_op | source)
XLA Modules:
  0.0 208.5 jit_solution(6033768300656926252)
XLA Ops:
  0.8 2.9 %broadcast_in_dim.42 = bf16[1024,2,128]{2,1,0:T(2,128)(2,1)S(1)} broadcast(bf16[1024,2]{1,0:T(8,128)(2,1)S(1)} %bitcast.102), dimensions={0,1} | broadcast | bytes 528384 | tf_op jit(solution)/shard_map/broadcast_in_dim | solution.py:36
  8.8 5.2 %collective-permute-start.1 = (bf16[16,32,512]{2,1,0:T(8,128)(2,1)S(1)}, bf16[16,32,512]{2,1,0:T(8,128)(2,1)S(1)}, u32[]{:S(2)}, u32[]{:S(2)}) collective-permute-start(bf16[16,32,512]{2,1,0:T(8,128)(2,1)S(1)} %maximum_select_fusion), channel_id=1, source_target_pairs={{1,0},{0,1},{3,2},{2,3},{5,4},{4,5},{7,6},{6,7},{9,8},{8,9},{11,10... | collective-permute-start | bytes 1572872 | tf_op jit(solution)/shard_map/ppermute | solution.py:52
  14.0 7.6 %all-to-all-start = ((bf16[32,32,256]{2,1,0:T(8,128)(2,1)}), bf16[32,32,256]{2,1,0:T(8,128)(2,1)}, u32[]{:S(2)}, u32[]{:S(2)}) async-start(bf16[32,32,256]{2,1,0:T(8,128)(2,1)} %bitcast.1), calls=%async_computation | async-start | bytes 1048576 | tf_op jit(solution)/shard_map/all_to_all | solution.py:54
  21.6 18.2 %collective-permute-done.1 = bf16[16,32,512]{2,1,0:T(8,128)(2,1)S(1)} collective-permute-done((bf16[16,32,512]{2,1,0:T(8,128)(2,1)S(1)}, bf16[16,32,512]{2,1,0:T(8,128)(2,1)S(1)}, u32[]{:S(2)}, u32[]{:S(2)}) %collective-permute-start.1) | collective-permute-done | bytes 524320 | tf_op jit(solution)/shard_map/ppermute | solution.py:52
  41.0 2.7 %collective-permute-start.2 = (bf16[2,16,32,512]{3,2,1,0:T(8,128)(2,1)}, bf16[2,16,32,512]{3,2,1,0:T(8,128)(2,1)S(1)}, u32[]{:S(2)}, u32[]{:S(2)}) collective-permute-start(bf16[2,16,32,512]{3,2,1,0:T(8,128)(2,1)} %pad_maximum_fusion), channel_id=1, source_target_pairs={{2,0},{3,1},{4,2},{5,3},{6,4},{7,5},{0,6},{1,7},{10,8},{11,9},{12,... | collective-permute-start | bytes 3145736 | tf_op jit(solution)/shard_map/ppermute | solution.py:64
  44.6 4.6 %all-to-all-done = bf16[32,32,256]{2,1,0:T(8,128)(2,1)} async-done(((bf16[32,32,256]{2,1,0:T(8,128)(2,1)}), bf16[32,32,256]{2,1,0:T(8,128)(2,1)}, u32[]{:S(2)}, u32[]{:S(2)}) %all-to-all-start) | async-done | bytes 524320 | tf_op jit(solution)/shard_map/all_to_all | solution.py:54
  53.6 4.7 %all-to-all-start.1 = ((bf16[8,32,1024]{2,1,0:T(8,128)(2,1)}), bf16[8,32,1024]{2,1,0:T(8,128)(2,1)}, u32[]{:S(2)}, u32[]{:S(2)}) async-start(bf16[8,32,1024]{2,1,0:T(8,128)(2,1)} %bitcast.99), calls=%async_computation.1 | async-start | bytes 1048576 | tf_op jit(solution)/shard_map/all_to_all | solution.py:59
  58.3 6.3 %collective-permute-done.2 = bf16[2,16,32,512]{3,2,1,0:T(8,128)(2,1)S(1)} collective-permute-done((bf16[2,16,32,512]{3,2,1,0:T(8,128)(2,1)}, bf16[2,16,32,512]{3,2,1,0:T(8,128)(2,1)S(1)}, u32[]{:S(2)}, u32[]{:S(2)}) %collective-permute-start.2) | collective-permute-done | bytes 1048608 | tf_op jit(solution)/shard_map/ppermute | solution.py:64
  65.5 3.4 %collective-permute-start.3 = (bf16[16,32,512]{2,1,0:T(8,128)(2,1)}, bf16[16,32,512]{2,1,0:T(8,128)(2,1)}, u32[]{:S(2)}, u32[]{:S(2)}) collective-permute-start(bf16[16,32,512]{2,1,0:T(8,128)(2,1)} %slice_bitcast_fusion.1), channel_id=1, source_target_pairs={{2,0},{3,1},{4,2},{5,3},{6,4},{7,5},{0,6},{1,7},{10,8},{11,9},{12,... | collective-permute-start | bytes 1572872 | tf_op jit(solution)/shard_map/ppermute | solution.py:66
  69.7 2.5 %broadcast_in_dim.45 = bf16[4,2,16,32,512]{4,3,2,1,0:T(8,128)(2,1)} broadcast(bf16[]{:T(256)} %constant.238.clone.1), dimensions={} | broadcast | bytes 4194306 | tf_op jit(solution)/shard_map/broadcast_in_dim | solution.py:69
  74.3 3.5 %collective-permute-start.20 = (bf16[256,1024]{1,0:T(8,128)(2,1)}, bf16[256,1024]{1,0:T(8,128)(2,1)S(1)}, u32[]{:S(2)}, u32[]{:S(2)}) collective-permute-start(bf16[256,1024]{1,0:T(8,128)(2,1)} %bitcast.4), channel_id=1, source_target_pairs={{128,0},{136,8},{144,16},{152,24},{160,32},{168,40},{176,48},{184,... | collective-permute-start | bytes 1572872 | tf_op jit(solution)/shard_map/ppermute | solution.py:85
  77.8 2.5 %collective-permute-start.15 = (bf16[256,1024]{1,0:T(8,128)(2,1)}, bf16[256,1024]{1,0:T(8,128)(2,1)S(1)}, u32[]{:S(2)}, u32[]{:S(2)}) collective-permute-start(bf16[256,1024]{1,0:T(8,128)(2,1)} %bitcast.4), channel_id=1, source_target_pairs={{192,0},{200,8},{208,16},{216,24},{224,32},{232,40},{240,48},{248,... | collective-permute-start | bytes 1572872 | tf_op jit(solution)/shard_map/ppermute | solution.py:85
  80.3 3.7 %collective-permute-start.7 = (bf16[256,1024]{1,0:T(8,128)(2,1)}, bf16[256,1024]{1,0:T(8,128)(2,1)S(1)}, u32[]{:S(2)}, u32[]{:S(2)}) collective-permute-start(bf16[256,1024]{1,0:T(8,128)(2,1)} %bitcast.4), channel_id=1, source_target_pairs={{48,0},{56,8},{0,16},{8,24},{16,32},{24,40},{32,48},{40,56},{112,6... | collective-permute-start | bytes 1572872 | tf_op jit(solution)/shard_map/ppermute | solution.py:87
  94.4 3.4 %collective-permute-start.9 = (bf16[128,1024]{1,0:T(8,128)(2,1)S(1)}, bf16[128,1024]{1,0:T(8,128)(2,1)S(1)}, u32[]{:S(2)}, u32[]{:S(2)}) collective-permute-start(bf16[128,1024]{1,0:T(8,128)(2,1)S(1)} %slice.109), channel_id=1, source_target_pairs={{48,0},{56,8},{0,16},{8,24},{16,32},{24,40},{32,48},{40,56},{112,6... | collective-permute-start | bytes 786440 | tf_op jit(solution)/shard_map/ppermute | solution.py:89
  97.9 12.0 %collective-permute-done.20 = bf16[256,1024]{1,0:T(8,128)(2,1)S(1)} collective-permute-done((bf16[256,1024]{1,0:T(8,128)(2,1)}, bf16[256,1024]{1,0:T(8,128)(2,1)S(1)}, u32[]{:S(2)}, u32[]{:S(2)}) %collective-permute-start.20) | collective-permute-done | bytes 524320 | tf_op jit(solution)/shard_map/ppermute | solution.py:85
  113.7 10.4 %collective-permute-done.15 = bf16[256,1024]{1,0:T(8,128)(2,1)S(1)} collective-permute-done((bf16[256,1024]{1,0:T(8,128)(2,1)}, bf16[256,1024]{1,0:T(8,128)(2,1)S(1)}, u32[]{:S(2)}, u32[]{:S(2)}) %collective-permute-start.15) | collective-permute-done | bytes 524320 | tf_op jit(solution)/shard_map/ppermute | solution.py:85
  124.9 4.2 %collective-permute-start.17 = (bf16[256,1024]{1,0:T(8,128)(2,1)S(1)}, bf16[256,1024]{1,0:T(8,128)(2,1)S(1)}, u32[]{:S(2)}, u32[]{:S(2)}) collective-permute-start(bf16[256,1024]{1,0:T(8,128)(2,1)S(1)} %collective-permute-done.15), channel_id=1, source_target_pairs={{48,0},{56,8},{0,16},{8,24},{16,32},{24,40},{32,48},{40,56},{112,6... | collective-permute-start | bytes 1572872 | tf_op jit(solution)/shard_map/ppermute | solution.py:87
  129.7 2.7 %collective-permute-start.12 = (bf16[256,1024]{1,0:T(8,128)(2,1)S(1)}, bf16[256,1024]{1,0:T(8,128)(2,1)S(1)}, u32[]{:S(2)}, u32[]{:S(2)}) collective-permute-start(bf16[256,1024]{1,0:T(8,128)(2,1)S(1)} %collective-permute-done.10), channel_id=1, source_target_pairs={{48,0},{56,8},{0,16},{8,24},{16,32},{24,40},{32,48},{40,56},{112,6... | collective-permute-start | bytes 1572872 | tf_op jit(solution)/shard_map/ppermute | solution.py:87
  136.0 4.4 %collective-permute-done.21 = bf16[256,1024]{1,0:T(8,128)(2,1)S(1)} collective-permute-done((bf16[256,1024]{1,0:T(8,128)(2,1)S(1)}, bf16[256,1024]{1,0:T(8,128)(2,1)S(1)}, u32[]{:S(2)}, u32[]{:S(2)}) %collective-permute-start.21) | collective-permute-done | bytes 524320 | tf_op jit(solution)/shard_map/ppermute | solution.py:86
  142.0 9.6 %collective-permute-done.16 = bf16[256,1024]{1,0:T(8,128)(2,1)S(1)} collective-permute-done((bf16[256,1024]{1,0:T(8,128)(2,1)S(1)}, bf16[256,1024]{1,0:T(8,128)(2,1)S(1)}, u32[]{:S(2)}, u32[]{:S(2)}) %collective-permute-start.16) | collective-permute-done | bytes 524320 | tf_op jit(solution)/shard_map/ppermute | solution.py:86
  153.5 9.4 %collective-permute-done.11 = bf16[256,1024]{1,0:T(8,128)(2,1)S(1)} collective-permute-done((bf16[256,1024]{1,0:T(8,128)(2,1)S(1)}, bf16[256,1024]{1,0:T(8,128)(2,1)S(1)}, u32[]{:S(2)}, u32[]{:S(2)}) %collective-permute-start.11) | collective-permute-done | bytes 524320 | tf_op jit(solution)/shard_map/ppermute | solution.py:86
  177.1 2.5 %collective-permute-done.13 = bf16[128,1024]{1,0:T(8,128)(2,1)S(1)} collective-permute-done((bf16[128,1024]{1,0:T(8,128)(2,1)S(1)}, bf16[128,1024]{1,0:T(8,128)(2,1)S(1)}, u32[]{:S(2)}, u32[]{:S(2)}) %collective-permute-start.13) | collective-permute-done | bytes 262176 | tf_op jit(solution)/shard_map/ppermute | solution.py:88
  186.9 11.6 %add_add_fusion = f32[1024,512]{1,0:T(8,128)} fusion(f32[1024,512]{1,0:T(8,128)} %fusion.21, f32[1024,512]{1,0:T(8,128)} %fusion.20, f32[1024,512]{1,0:T(8,128)} %fusion.19, f32[1024,512]{1,0:T(8,128)S(1)} %fusion.18, f32[1024,512]{1,0:T(8,128)} %fusion.17, f32[1024,512]{1,0:T(8,128)} %fusion.16, f32[1024,512]{1,0:T(8,128)} %fusion.15, ...), kind=kOutput, calls=%fused_computation.2 | convolution fusion | flops 278396928 | bytes 42729472 | tf_op jit(solution)/shard_map/dot_general | solution.py:30
  199.9 3.7 %collective-permute-start.25 = (f32[1024,256]{1,0:T(8,128)S(1)}, f32[1024,256]{1,0:T(8,128)}, u32[]{:S(2)}, u32[]{:S(2)}) collective-permute-start(f32[1024,256]{1,0:T(8,128)S(1)} %constant_dynamic-slice_fusion.4), channel_id=1, source_target_pairs={{8,0},{0,8},{24,16},{16,24},{40,32},{32,40},{56,48},{48,56},{72,64... | collective-permute-start | bytes 3145736 | tf_op jit(solution)/shard_map/ppermute | solution.py:97
  (96 shorter events, 66.6 us)
Async XLA Ops:
  8.8 31.0 %collective-permute-start.1 = (bf16[16,32,512]{2,1,0:T(8,128)(2,1)S(1)}, bf16[16,32,512]{2,1,0:T(8,128)(2,1)S(1)}, u32[]{:S(2)}, u32[]{:S(2)}) collective-permute-start(bf16[16,32,512]{2,1,0:T(8,128)(2,1)S(1)} %maximum_select_fusion), channel_id=1, source_target_pairs={{1,0},{0,1},{3,2},{2,3},{5,4},{4,5},{7,6},{6,7},{9,8},{8,9},{11,10... | collective-permute-start | bytes 1572872 | tf_op jit(solution)/shard_map/ppermute | solution.py:52
  14.0 35.1 %all-to-all-start = ((bf16[32,32,256]{2,1,0:T(8,128)(2,1)}), bf16[32,32,256]{2,1,0:T(8,128)(2,1)}, u32[]{:S(2)}, u32[]{:S(2)}) async-start(bf16[32,32,256]{2,1,0:T(8,128)(2,1)} %bitcast.1), calls=%async_computation | async-start | bytes 1048576 | tf_op jit(solution)/shard_map/all_to_all | solution.py:54
  41.0 23.6 %collective-permute-start.2 = (bf16[2,16,32,512]{3,2,1,0:T(8,128)(2,1)}, bf16[2,16,32,512]{3,2,1,0:T(8,128)(2,1)S(1)}, u32[]{:S(2)}, u32[]{:S(2)}) collective-permute-start(bf16[2,16,32,512]{3,2,1,0:T(8,128)(2,1)} %pad_maximum_fusion), channel_id=1, source_target_pairs={{2,0},{3,1},{4,2},{5,3},{6,4},{7,5},{0,6},{1,7},{10,8},{11,9},{12,... | collective-permute-start | bytes 3145736 | tf_op jit(solution)/shard_map/ppermute | solution.py:64
  44.4 24.5 %collective-permute-start.4 = (bf16[2,16,32,512]{3,2,1,0:T(8,128)(2,1)}, bf16[2,16,32,512]{3,2,1,0:T(8,128)(2,1)S(1)}, u32[]{:S(2)}, u32[]{:S(2)}) collective-permute-start(bf16[2,16,32,512]{3,2,1,0:T(8,128)(2,1)} %pad_maximum_fusion), channel_id=1, source_target_pairs={{6,0},{7,1},{0,2},{1,3},{2,4},{3,5},{4,6},{5,7},{14,8},{15,9},{8,1... | collective-permute-start | bytes 3145736 | tf_op jit(solution)/shard_map/ppermute | solution.py:65
  53.6 20.6 %all-to-all-start.1 = ((bf16[8,32,1024]{2,1,0:T(8,128)(2,1)}), bf16[8,32,1024]{2,1,0:T(8,128)(2,1)}, u32[]{:S(2)}, u32[]{:S(2)}) async-start(bf16[8,32,1024]{2,1,0:T(8,128)(2,1)} %bitcast.99), calls=%async_computation.1 | async-start | bytes 1048576 | tf_op jit(solution)/shard_map/all_to_all | solution.py:59
  65.5 14.9 %collective-permute-start.3 = (bf16[16,32,512]{2,1,0:T(8,128)(2,1)}, bf16[16,32,512]{2,1,0:T(8,128)(2,1)}, u32[]{:S(2)}, u32[]{:S(2)}) collective-permute-start(bf16[16,32,512]{2,1,0:T(8,128)(2,1)} %slice_bitcast_fusion.1), channel_id=1, source_target_pairs={{2,0},{3,1},{4,2},{5,3},{6,4},{7,5},{0,6},{1,7},{10,8},{11,9},{12,... | collective-permute-start | bytes 1572872 | tf_op jit(solution)/shard_map/ppermute | solution.py:66
  69.7 14.3 %collective-permute-start.5 = (bf16[16,32,512]{2,1,0:T(8,128)(2,1)}, bf16[16,32,512]{2,1,0:T(8,128)(2,1)}, u32[]{:S(2)}, u32[]{:S(2)}) collective-permute-start(bf16[16,32,512]{2,1,0:T(8,128)(2,1)} %slice_bitcast_fusion), channel_id=1, source_target_pairs={{6,0},{7,1},{0,2},{1,3},{2,4},{3,5},{4,6},{5,7},{14,8},{15,9},{8,1... | collective-permute-start | bytes 1572872 | tf_op jit(solution)/shard_map/ppermute | solution.py:67
  74.3 35.6 %collective-permute-start.20 = (bf16[256,1024]{1,0:T(8,128)(2,1)}, bf16[256,1024]{1,0:T(8,128)(2,1)S(1)}, u32[]{:S(2)}, u32[]{:S(2)}) collective-permute-start(bf16[256,1024]{1,0:T(8,128)(2,1)} %bitcast.4), channel_id=1, source_target_pairs={{128,0},{136,8},{144,16},{152,24},{160,32},{168,40},{176,48},{184,... | collective-permute-start | bytes 1572872 | tf_op jit(solution)/shard_map/ppermute | solution.py:85
  77.8 46.3 %collective-permute-start.15 = (bf16[256,1024]{1,0:T(8,128)(2,1)}, bf16[256,1024]{1,0:T(8,128)(2,1)S(1)}, u32[]{:S(2)}, u32[]{:S(2)}) collective-permute-start(bf16[256,1024]{1,0:T(8,128)(2,1)} %bitcast.4), channel_id=1, source_target_pairs={{192,0},{200,8},{208,16},{216,24},{224,32},{232,40},{240,48},{248,... | collective-permute-start | bytes 1572872 | tf_op jit(solution)/shard_map/ppermute | solution.py:85
  80.3 44.6 %collective-permute-start.10 = (bf16[256,1024]{1,0:T(8,128)(2,1)}, bf16[256,1024]{1,0:T(8,128)(2,1)S(1)}, u32[]{:S(2)}, u32[]{:S(2)}) collective-permute-start(bf16[256,1024]{1,0:T(8,128)(2,1)} %bitcast.4), channel_id=1, source_target_pairs={{64,0},{72,8},{80,16},{88,24},{96,32},{104,40},{112,48},{120,56},{... | collective-permute-start | bytes 1572872 | tf_op jit(solution)/shard_map/ppermute | solution.py:85
  80.3 14.0 %collective-permute-start.7 = (bf16[256,1024]{1,0:T(8,128)(2,1)}, bf16[256,1024]{1,0:T(8,128)(2,1)S(1)}, u32[]{:S(2)}, u32[]{:S(2)}) collective-permute-start(bf16[256,1024]{1,0:T(8,128)(2,1)} %bitcast.4), channel_id=1, source_target_pairs={{48,0},{56,8},{0,16},{8,24},{16,32},{24,40},{32,48},{40,56},{112,6... | collective-permute-start | bytes 1572872 | tf_op jit(solution)/shard_map/ppermute | solution.py:87
  94.4 35.2 %collective-permute-start.9 = (bf16[128,1024]{1,0:T(8,128)(2,1)S(1)}, bf16[128,1024]{1,0:T(8,128)(2,1)S(1)}, u32[]{:S(2)}, u32[]{:S(2)}) collective-permute-start(bf16[128,1024]{1,0:T(8,128)(2,1)S(1)} %slice.109), channel_id=1, source_target_pairs={{48,0},{56,8},{0,16},{8,24},{16,32},{24,40},{32,48},{40,56},{112,6... | collective-permute-start | bytes 786440 | tf_op jit(solution)/shard_map/ppermute | solution.py:89
  97.8 31.9 %collective-permute-start.8 = (bf16[128,1024]{1,0:T(8,128)(2,1)S(1)}, bf16[128,1024]{1,0:T(8,128)(2,1)S(1)}, u32[]{:S(2)}, u32[]{:S(2)}) collective-permute-start(bf16[128,1024]{1,0:T(8,128)(2,1)S(1)} %slice.108), channel_id=1, source_target_pairs={{16,0},{24,8},{32,16},{40,24},{48,32},{56,40},{0,48},{8,56},{80,64... | collective-permute-start | bytes 786440 | tf_op jit(solution)/shard_map/ppermute | solution.py:88
  109.9 22.5 %collective-permute-start.22 = (bf16[256,1024]{1,0:T(8,128)(2,1)S(1)}, bf16[256,1024]{1,0:T(8,128)(2,1)S(1)}, u32[]{:S(2)}, u32[]{:S(2)}) collective-permute-start(bf16[256,1024]{1,0:T(8,128)(2,1)S(1)} %collective-permute-done.20), channel_id=1, source_target_pairs={{48,0},{56,8},{0,16},{8,24},{16,32},{24,40},{32,48},{40,56},{112,6... | collective-permute-start | bytes 1572872 | tf_op jit(solution)/shard_map/ppermute | solution.py:87
  124.1 16.3 %collective-permute-start.21 = (bf16[256,1024]{1,0:T(8,128)(2,1)S(1)}, bf16[256,1024]{1,0:T(8,128)(2,1)S(1)}, u32[]{:S(2)}, u32[]{:S(2)}) collective-permute-start(bf16[256,1024]{1,0:T(8,128)(2,1)S(1)} %collective-permute-done.20), channel_id=1, source_target_pairs={{16,0},{24,8},{32,16},{40,24},{48,32},{56,40},{0,48},{8,56},{80,64... | collective-permute-start | bytes 1572872 | tf_op jit(solution)/shard_map/ppermute | solution.py:86
  124.9 16.7 %collective-permute-start.17 = (bf16[256,1024]{1,0:T(8,128)(2,1)S(1)}, bf16[256,1024]{1,0:T(8,128)(2,1)S(1)}, u32[]{:S(2)}, u32[]{:S(2)}) collective-permute-start(bf16[256,1024]{1,0:T(8,128)(2,1)S(1)} %collective-permute-done.15), channel_id=1, source_target_pairs={{48,0},{56,8},{0,16},{8,24},{16,32},{24,40},{32,48},{40,56},{112,6... | collective-permute-start | bytes 1572872 | tf_op jit(solution)/shard_map/ppermute | solution.py:87
  129.6 22.1 %collective-permute-start.16 = (bf16[256,1024]{1,0:T(8,128)(2,1)S(1)}, bf16[256,1024]{1,0:T(8,128)(2,1)S(1)}, u32[]{:S(2)}, u32[]{:S(2)}) collective-permute-start(bf16[256,1024]{1,0:T(8,128)(2,1)S(1)} %collective-permute-done.15), channel_id=1, source_target_pairs={{16,0},{24,8},{32,16},{40,24},{48,32},{56,40},{0,48},{8,56},{80,64... | collective-permute-start | bytes 1572872 | tf_op jit(solution)/shard_map/ppermute | solution.py:86
  129.7 23.1 %collective-permute-start.12 = (bf16[256,1024]{1,0:T(8,128)(2,1)S(1)}, bf16[256,1024]{1,0:T(8,128)(2,1)S(1)}, u32[]{:S(2)}, u32[]{:S(2)}) collective-permute-start(bf16[256,1024]{1,0:T(8,128)(2,1)S(1)} %collective-permute-done.10), channel_id=1, source_target_pairs={{48,0},{56,8},{0,16},{8,24},{16,32},{24,40},{32,48},{40,56},{112,6... | collective-permute-start | bytes 1572872 | tf_op jit(solution)/shard_map/ppermute | solution.py:87
  132.3 30.5 %collective-permute-start.11 = (bf16[256,1024]{1,0:T(8,128)(2,1)S(1)}, bf16[256,1024]{1,0:T(8,128)(2,1)S(1)}, u32[]{:S(2)}, u32[]{:S(2)}) collective-permute-start(bf16[256,1024]{1,0:T(8,128)(2,1)S(1)} %collective-permute-done.10), channel_id=1, source_target_pairs={{16,0},{24,8},{32,16},{40,24},{48,32},{56,40},{0,48},{8,56},{80,64... | collective-permute-start | bytes 1572872 | tf_op jit(solution)/shard_map/ppermute | solution.py:86
  140.4 41.0 %collective-permute-start.24 = (bf16[128,1024]{1,0:T(8,128)(2,1)S(1)}, bf16[128,1024]{1,0:T(8,128)(2,1)S(1)}, u32[]{:S(2)}, u32[]{:S(2)}) collective-permute-start(bf16[128,1024]{1,0:T(8,128)(2,1)S(1)} %slice.115), channel_id=1, source_target_pairs={{48,0},{56,8},{0,16},{8,24},{16,32},{24,40},{32,48},{40,56},{112,6... | collective-permute-start | bytes 786440 | tf_op jit(solution)/shard_map/ppermute | solution.py:89
  141.6 31.5 %collective-permute-start.23 = (bf16[128,1024]{1,0:T(8,128)(2,1)S(1)}, bf16[128,1024]{1,0:T(8,128)(2,1)S(1)}, u32[]{:S(2)}, u32[]{:S(2)}) collective-permute-start(bf16[128,1024]{1,0:T(8,128)(2,1)S(1)} %slice.114), channel_id=1, source_target_pairs={{16,0},{24,8},{32,16},{40,24},{48,32},{56,40},{0,48},{8,56},{80,64... | collective-permute-start | bytes 786440 | tf_op jit(solution)/shard_map/ppermute | solution.py:88
  151.6 31.5 %collective-permute-start.19 = (bf16[128,1024]{1,0:T(8,128)(2,1)S(1)}, bf16[128,1024]{1,0:T(8,128)(2,1)S(1)}, u32[]{:S(2)}, u32[]{:S(2)}) collective-permute-start(bf16[128,1024]{1,0:T(8,128)(2,1)S(1)} %slice.113), channel_id=1, source_target_pairs={{48,0},{56,8},{0,16},{8,24},{16,32},{24,40},{32,48},{40,56},{112,6... | collective-permute-start | bytes 786440 | tf_op jit(solution)/shard_map/ppermute | solution.py:89
  152.8 22.4 %collective-permute-start.18 = (bf16[128,1024]{1,0:T(8,128)(2,1)S(1)}, bf16[128,1024]{1,0:T(8,128)(2,1)S(1)}, u32[]{:S(2)}, u32[]{:S(2)}) collective-permute-start(bf16[128,1024]{1,0:T(8,128)(2,1)S(1)} %slice.112), channel_id=1, source_target_pairs={{16,0},{24,8},{32,16},{40,24},{48,32},{56,40},{0,48},{8,56},{80,64... | collective-permute-start | bytes 786440 | tf_op jit(solution)/shard_map/ppermute | solution.py:88
  162.9 22.1 %collective-permute-start.14 = (bf16[128,1024]{1,0:T(8,128)(2,1)S(1)}, bf16[128,1024]{1,0:T(8,128)(2,1)S(1)}, u32[]{:S(2)}, u32[]{:S(2)}) collective-permute-start(bf16[128,1024]{1,0:T(8,128)(2,1)S(1)} %slice.111), channel_id=1, source_target_pairs={{48,0},{56,8},{0,16},{8,24},{16,32},{24,40},{32,48},{40,56},{112,6... | collective-permute-start | bytes 786440 | tf_op jit(solution)/shard_map/ppermute | solution.py:89
  (7 other events, 61.5 us)

commit v2 on v0

v2 whole, which is shorter than its diff:
```python
import functools

import jax
import jax.numpy as jnp
from jax import lax
from jax.experimental import pallas as pl
from jax.experimental.pallas import tpu as pltpu
from jax.sharding import Mesh, PartitionSpec as P

TILE = 128
SIZES = {"zl": 4, "x": 4, "c": 2, "y": 4, "zh": 2}
BLK = ("zl", "x", "c")
USERS = ("y", "zh")
LINE = ("zl", "zh")
VMEM = pl.BlockSpec(memory_space=pltpu.VMEM)
SMEM = pl.BlockSpec(memory_space=pltpu.SMEM)
LIMIT = 48 * 1024 * 1024
ROWS = ((0, 512), (512, 512))
GROUPS = ((0, 1, -1, 2, -2), (3, -3, 4))
TAIL = 16
LARGEST = 32768.0


def shift(a, axis, by):
    n = SIZES[axis]
    return lax.ppermute(a, axis, [((i + by) % n, i) for i in range(n)])


def along(a, by):
    n = SIZES["zh"] * SIZES["zl"]
    index = [i % SIZES["zl"] * SIZES["zh"] + i // SIZES["zl"] for i in range(n)]
    return lax.ppermute(a, LINE, [(index[(i + by) % n], index[i]) for i in range(n)])


def tie(a, *others):
    return lax.optimization_barrier((a, *others))[0]


def mask_kernel(core, tiles, full, blocks, ordered):
    rows, width = full.shape
    nz, nx = SIZES["zl"], SIZES["x"]
    piece = blocks.shape[1]
    c = core[0]
    for i in range(rows // TILE):
        for j in range(width // TILE):
            kept = tiles[i, j].astype(jnp.float32).astype(full.dtype)
            cols = pl.ds(j * TILE, TILE)
            value = full[pl.ds(i * TILE, TILE), cols] * kept
            for k in range(TILE // piece):
                t = i * (TILE // piece) + k
                x, z, e = t // (nz * 2), t // 2 % nz, t % 2
                part = value[k * piece:(k + 1) * piece]
                blocks[(z * nx + x) * 2 + e, :, cols] = part
                ordered[x, c ^ e, pl.ds(z * piece, piece), cols] = part


def apply_mask(interactions, tile_mask, core, panels):
    rows, width = interactions.shape
    piece = rows // panels
    nx = SIZES["x"]
    return pl.pallas_call(
        mask_kernel,
        out_shape=(
            jax.ShapeDtypeStruct((panels, piece, width), interactions.dtype),
            jax.ShapeDtypeStruct((nx, 2, rows // nx // 2, width), interactions.dtype),
        ),
        in_specs=[SMEM, SMEM, VMEM],
        out_specs=(VMEM, VMEM),
        name="mask",
    )(core, tile_mask, interactions)


def pick_kernel(order, spread, out):
    per, width = out.shape[3] // spread.shape[2], spread.shape[2]
    for y in range(SIZES["y"]):
        for h in range(SIZES["zh"]):
            for p in range(per):
                at = (y * SIZES["zh"] + h) * per + p
                out[y, h, :, p * width:(p + 1) * width] = spread[order[at]]


def pick(order, spread):
    panels, piece, width = spread.shape
    users = SIZES["y"] * SIZES["zh"]
    return pl.pallas_call(
        pick_kernel,
        out_shape=jax.ShapeDtypeStruct(
            (SIZES["y"], SIZES["zh"], piece, panels // users * width), spread.dtype
        ),
        in_specs=[SMEM, VMEM],
        out_specs=VMEM,
        name="pick",
    )(order, spread)


def product_kernel(groups, n_near, at, *refs):
    nx, ny = SIZES["x"], SIZES["y"]
    sides, refs = refs[:2 * len(groups)], refs[2 * len(groups):]
    near, away, outs = refs[:n_near], refs[n_near:-nx], refs[-nx:]

    def column(refs, dy, here):
        return refs[dy][here] if len(refs) > 1 else refs[0][(at[dy], *here)]

    piece = sides[0].shape[2]
    rows, cols = [], []
    chunk = 0
    for g, size in enumerate(groups):
        for k in range(size):
            low = pl.multiple_of(at[ny + 2 * chunk] * piece, piece)
            same = at[ny + 2 * chunk + 1] == 0
            chunk += 1
            for crel in range(2):
                for dy in range(ny):
                    rows.append(sides[2 * g + crel][k, at[dy]])
                    here = (slice(None), crel, pl.ds(low, piece))
                    cols.append(jnp.where(same, column(near, dy, here), column(away, dy, here)))
    rows = jnp.concatenate(rows, 0).T
    for dx in range(nx):
        b = jnp.concatenate([c[dx] for c in cols], 0)
        r = jnp.dot(rows, b, preferred_element_type=jnp.float32)
        if dx == 0:
            outs[dx][...] = r
            continue
        most = jnp.maximum(jnp.max(jnp.abs(r)), 1e-30)
        power = jnp.floor(jnp.log2(jnp.full((TAIL, r.shape[1]), LARGEST / most, jnp.float32)))
        outs[dx][0, :r.shape[0]] = r * jnp.exp2(power[:1])
        outs[dx][0, r.shape[0]:] = power


def product(at, sides, near, away, lo, size):
    _, ny, piece, _ = sides[0].shape
    nx, width = SIZES["x"], near[0].shape[-1]
    tile = 256
    groups = tuple(a.shape[0] for a in sides[::2])
    n_chunks = sum(groups)
    in_specs = [
        pl.BlockSpec((a.shape[0], ny, piece, tile), lambda i, s: (0, 0, 0, i + lo // tile)) for a in sides
    ]
    for a in (*near, *away):
        in_specs.append(pl.BlockSpec(a.shape, functools.partial(lambda n, i, s: (0,) * n, a.ndim)))
    plain = jax.ShapeDtypeStruct((size, width), jnp.float32)
    packed = jax.ShapeDtypeStruct((size // tile, tile + TAIL, width), jnp.float32)
    depth = 2 * n_chunks * ny * piece
    return pl.pallas_call(
        functools.partial(product_kernel, groups, len(near)),
        out_shape=(plain,) + (packed,) * (nx - 1),
        grid_spec=pltpu.PrefetchScalarGridSpec(
            num_scalar_prefetch=1,
            grid=(size // tile,),
            in_specs=in_specs,
            out_specs=(pl.BlockSpec((tile, width), lambda i, s: (i, 0)),)
            + (pl.BlockSpec((1, tile + TAIL, width), lambda i, s: (i, 0, 0)),) * (nx - 1),
        ),
        compiler_params=pltpu.CompilerParams(vmem_limit_bytes=LIMIT),
        cost_estimate=pl.CostEstimate(
            flops=2 * depth * size * nx * width,
            bytes_accessed=2 * depth * size + 4096 * nx * width + 4 * nx * size * width,
            transcendentals=0,
        ),
        name="product",
    )(at, *sides, *near, *away)


def opened(message):
    tiles, rows, width = message.shape
    body = message[:, :rows - TAIL].astype(jnp.float32)
    power = message[:, rows - TAIL:rows - TAIL + 1].astype(jnp.float32)
    return (body * jnp.exp2(-power)).reshape(tiles * (rows - TAIL), width)


def on_device(interactions, tile_mask, panel_of):
    rows, width = interactions.shape
    panels = panel_of.shape[0]
    x, core, y, zh, zl = (lax.axis_index(name) for name in ("x", "c", "y", "zh", "zl"))
    nx, ny, nz = SIZES["x"], SIZES["y"], SIZES["zl"]
    around = SIZES["zh"] * nz
    ring = zh * nz + zl

    blocks, ordered = apply_mask(interactions, tile_mask, core.reshape(1).astype(jnp.int32), panels)
    spread = lax.all_to_all(blocks, BLK, 0, 0, tiled=True)

    def over_x(a, *after):
        def slice_for(dx):
            return lax.dynamic_index_in_dim(a, (x + dx) % nx, 0, keepdims=False)

        return jnp.stack(
            [slice_for(0)] + [shift(tie(slice_for(-dx), *after), "x", dx) for dx in range(1, nx)], 0
        )

    mine = over_x(ordered)
    near = [mine] + [shift(mine, "y", dy) for dy in range(1, ny)]
    crossed = shift(mine, "zh", 1)
    across = crossed
    away = [lax.all_to_all(jnp.broadcast_to(across[None], (ny, *across.shape)), "y", 0, 0)]

    stored = jnp.arange(panels, dtype=jnp.int32)
    order = jnp.sum(jnp.where(panel_of[None, :] == stored[:, None], stored[None, :], 0), 1).astype(jnp.int32)
    mixed = lax.all_to_all(pick(order, tie(spread, mine)), "y", 0, 0, tiled=True)
    flat = (-1, mixed.shape[-1])

    def side(h):
        return lax.dynamic_index_in_dim(mixed, h, 1, keepdims=False)

    def from_ring(d, *after):
        if d == 0:
            return side(zh)
        dest = (ring - d) % around
        part = side(dest // nz)
        return along(tie(part.reshape(flat), *after), d).reshape(part.shape)

    def where():
        out = [(y + dy) % ny for dy in range(ny)]
        for group in GROUPS:
            for d in group:
                source = (ring + d) % around
                out += [source % nz, (source // nz) ^ zh]
        return jnp.stack(out).astype(jnp.int32)

    held = {0: from_ring(0)}
    for d in (1, -1):
        held[d] = from_ring(d)
    for d in (2, -2):
        held[d] = from_ring(d, across)
    for d in (3, -3):
        held[d] = from_ring(d, across, held[1], held[-1])
    for d in (4,):
        held[d] = from_ring(d, held[1], held[-1], *near)
    sides = []
    for group in GROUPS:
        own = jnp.stack([held[d] for d in group], 0)
        sides += [own, shift(own, "c", 1)]
    done = []
    for lo, size in ROWS:
        total, *sent = product(where(), sides, near, away, lo, size)
        for dx in range(1, nx):
            total = total + opened(shift(sent[dx - 1].astype(jnp.float16), "x", -dx))
        done.append(total)
    return jnp.concatenate(done, 0)


def solution(mesh):
    fine = Mesh(mesh.devices.reshape(tuple(SIZES.values())), tuple(SIZES))
    return jax.shard_map(
        on_device,
        mesh=fine,
        in_specs=(P(USERS, BLK), P(USERS, BLK), P()),
        out_specs=P(USERS, BLK),
        check_vma=False,
    )
```

time: 441 us -> 166 us (0.38)
  waiting for transfers between devices: 312 us -> 73.8 us
  local copies, waits for them, and re-layouts: 76.4 us -> 10.5 us
  starting transfers between devices: 0.04 us -> 63.5 us
  loops' own time: 21.3 us -> 0 us
  Pallas kernels: 0 us -> 15.1 us
  matrix products: 13.8 us -> 0 us
  between operations: 13.4 us -> 0.39 us
    reduce_scatter x1 -> x0, waiting for transfers between devices: 185 us -> none  [on_device(): lax.psum_scatter(partial_rows, 'users', scatter_dimension=0, tiled=True)]
    all_gather x1 -> x0, waiting for transfers between devices: 128 us -> none  [on_device(): piece = lax.all_gather(masked, 'blk', axis=1, tiled=True)]
    ppermute x0 -> x22, waiting for transfers between devices: none -> 67.2 us  [the longest x15 38.8 us: shift(): return lax.ppermute(a, axis, [((i + by) % n, i) for i in range(n)])]
    dynamic_update_slice x32 -> x0, local copies, waits for them, and re-layouts: 53.6 us -> none  [put_panel(): return lax.dynamic_update_slice_in_dim(total, rows_block, target, 0)]
    ppermute x0 -> x22, starting transfers between devices: none -> 44.8 us  [the longest x15 27.5 us: shift(): return lax.ppermute(a, axis, [((i + by) % n, i) for i in range(n)])]
    another operation x1 -> x0, loops' own time: 21.3 us -> none  [on_device(): partial_rows = lax.fori_loop(0, stored_count, put_panel, empty)]
    all_to_all x0 -> x3, starting transfers between devices: none -> 18.8 us  [the longest x1 10.2 us: on_device(): spread = lax.all_to_all(blocks, BLK, 0, 0, tiled=True)]
    dynamic_slice x32 -> x2, local copies, waits for them, and re-layouts: 18.6 us -> 1.2 us  [the longest x1 1.15 us: side(): return lax.dynamic_index_in_dim(mixed, h, 1, keepdims=False)]
  transfers between devices with their start and end apart: 2 -> 25, of which waited for: 2 -> 16; matrix products, arithmetic and copies ran while one was open for 0% -> 5% of each run, Pallas kernels for 0% -> 3%
where the time goes in v2:
time: 166 us
  waiting for transfers between devices  73.8 us (44%)
  starting transfers between devices  63.5 us (38%)
  Pallas kernels  15.1 us (9%)
  local copies, waits for them, and re-layouts  10.5 us (6%)
  other arithmetic  2.69 us (2%)
    ppermute x15, waiting for transfers between devices, shift(): return lax.ppermute(a, axis, [((i + by) % n, i) for i in range(n)])  38.8 us
    ppermute x7, waiting for transfers between devices, along(): lax.ppermute(a, LINE, [(index[(i + by) % n], index[i]) for i in range(n)])  28.4 us
    ppermute x15, starting transfers between devices, shift(): return lax.ppermute(a, axis, [((i + by) % n, i) for i in range(n)])  27.5 us
    ppermute x7, starting transfers between devices, along(): lax.ppermute(a, LINE, [(index[(i + by) % n], index[i]) for i in range(n)])  17.3 us
    pallas_call x2, Pallas kernels, product(): pl.pallas_call(functools.partial(product_kernel, groups, len(near)), out_...  11 us
    all_to_all x1, starting transfers between devices, on_device(): spread = lax.all_to_all(blocks, BLK, 0, 0, tiled=True)  10.2 us
    unnamed x25, local copies, waits for them, and re-layouts  6.87 us
    all_to_all x1, waiting for transfers between devices, on_device(): lax.all_to_all(pick(order, tie(spread, mine)), 'y', 0, 0, tiled=True)  5.46 us
  transfers between devices with their start and end apart: 25, of which 16 were waited for; matrix products, arithmetic and copies ran while one was open for 5% of the time, Pallas kernels for 3%

profile of v2, /device:TPU:1, one launch (start us, length us, event | category | flops | bytes accessed | tf_op | source)
XLA Modules:
  0.0 165.9 jit_solution(17744067364461940019)
XLA Ops:
  1.3 2.2 %mask.1 = (bf16[32,32,256]{2,1,0:T(8,128)(2,1)}, bf16[4,2,128,256]{3,2,1,0:T(8,128)(2,1)}) custom-call(s32[1]{0:T(128)} %bitcast.20.core, s32[8,2]{1,0:T(8,128)} %copy.5.tiles, bf16[1024,256]{1,0:T(8,128)(2,1)} %full.1), custom_call_target="tpu_custom_call" | custom-call | tf_op jit(solution)/shard_map/mask/pallas_call | solution.py:61
  3.5 10.2 %all-to-all-start = ((bf16[32,32,256]{2,1,0:T(8,128)(2,1)}), bf16[32,32,256]{2,1,0:T(8,128)(2,1)S(1)}, u32[]{:S(2)}, u32[]{:S(2)}) async-start(bf16[32,32,256]{2,1,0:T(8,128)(2,1)} %get-tuple-element.21), calls=%async_computation | async-start | bytes 1048576 | tf_op jit(solution)/shard_map/all_to_all | solution.py:180
  13.8 2.7 %collective-permute-start = (bf16[2,128,256]{2,1,0:T(8,128)(2,1)S(1)}, bf16[2,128,256]{2,1,0:T(8,128)(2,1)S(1)}, u32[]{:S(2)}, u32[]{:S(2)}) collective-permute-start(bf16[2,128,256]{2,1,0:T(8,128)(2,1)S(1)} %get-tuple-element.47), channel_id=1, source_target_pairs={{16,0},{32,16},{48,32},{0,48},{17,1},{33,17},{49,33},{1,49},{18,2}... | collective-permute-start | bytes 393224 | tf_op jit(solution)/shard_map/ppermute | solution.py:26
  18.3 4.6 %collective-permute-done = bf16[2,128,256]{2,1,0:T(8,128)(2,1)S(1)} collective-permute-done((bf16[2,128,256]{2,1,0:T(8,128)(2,1)S(1)}, bf16[2,128,256]{2,1,0:T(8,128)(2,1)S(1)}, u32[]{:S(2)}, u32[]{:S(2)}) %collective-permute-start) | collective-permute-done | bytes 131104 | tf_op jit(solution)/shard_map/ppermute | solution.py:26
  24.8 4.1 %collective-permute-done.2 = bf16[2,128,256]{2,1,0:T(8,128)(2,1)S(1)} collective-permute-done((bf16[2,128,256]{2,1,0:T(8,128)(2,1)S(1)}, bf16[2,128,256]{2,1,0:T(8,128)(2,1)S(1)}, u32[]{:S(2)}, u32[]{:S(2)}) %collective-permute-start.2) | collective-permute-done | bytes 131104 | tf_op jit(solution)/shard_map/ppermute | solution.py:26
  32.8 4.2 %all-to-all-start.1 = ((bf16[4,2,32,1024]{3,2,1,0:T(8,128)(2,1)}), bf16[4,2,32,1024]{3,2,1,0:T(8,128)(2,1)S(1)}, u32[]{:S(2)}, u32[]{:S(2)}) async-start(bf16[4,2,32,1024]{3,2,1,0:T(8,128)(2,1)} %pick.1), calls=%async_computation.1 | async-start | bytes 1048576 | tf_op jit(solution)/shard_map/all_to_all | solution.py:198
  36.9 4.2 %collective-permute-start.5 = (bf16[4,2,128,256]{3,2,1,0:T(8,128)(2,1)S(1)}, bf16[4,2,128,256]{3,2,1,0:T(8,128)(2,1)S(1)}, u32[]{:S(2)}, u32[]{:S(2)}) collective-permute-start(bf16[4,2,128,256]{3,2,1,0:T(8,128)(2,1)S(1)} %pad_maximum_fusion.2.refs_4_), channel_id=1, source_target_pairs={{1,0},{0,1},{3,2},{2,3},{5,4},{4,5},{7,6},{6,7},{9,8},{8,9},{11,10... | collective-permute-start | bytes 1572872 | tf_op jit(solution)/shard_map/ppermute | solution.py:26
  41.2 5.5 %all-to-all-done.1 = bf16[4,2,32,1024]{3,2,1,0:T(8,128)(2,1)S(1)} async-done(((bf16[4,2,32,1024]{3,2,1,0:T(8,128)(2,1)}), bf16[4,2,32,1024]{3,2,1,0:T(8,128)(2,1)S(1)}, u32[]{:S(2)}, u32[]{:S(2)}) %all-to-all-start.1) | async-done | bytes 524320 | tf_op jit(solution)/shard_map/all_to_all | solution.py:198
  47.8 2.3 %collective-permute-start.3 = (bf16[128,1024]{1,0:T(8,128)(2,1)}, bf16[128,1024]{1,0:T(8,128)(2,1)S(1)}, u32[]{:S(2)}, u32[]{:S(2)}) collective-permute-start(bf16[128,1024]{1,0:T(8,128)(2,1)} %bitcast.28), channel_id=1, source_target_pairs={{64,0},{128,64},{192,128},{1,192},{65,1},{129,65},{193,129},{0,193... | collective-permute-start | bytes 786440 | tf_op jit(solution)/shard_map/ppermute | solution.py:32
  52.1 7.9 %collective-permute-done.5 = bf16[4,2,128,256]{3,2,1,0:T(8,128)(2,1)S(1)} collective-permute-done((bf16[4,2,128,256]{3,2,1,0:T(8,128)(2,1)S(1)}, bf16[4,2,128,256]{3,2,1,0:T(8,128)(2,1)S(1)}, u32[]{:S(2)}, u32[]{:S(2)}) %collective-permute-start.5) | collective-permute-done | bytes 524320 | tf_op jit(solution)/shard_map/ppermute | solution.py:26
  61.6 4.4 %all-to-all-start.2 = ((bf16[4,4,2,128,256]{4,3,2,1,0:T(8,128)(2,1)}), bf16[4,4,2,128,256]{4,3,2,1,0:T(8,128)(2,1)}, u32[]{:S(2)}, u32[]{:S(2)}) async-start(bf16[4,4,2,128,256]{4,3,2,1,0:T(8,128)(2,1)} %broadcast_in_dim.23), calls=%async_computation.2 | async-start | bytes 4194304 | tf_op jit(solution)/shard_map/all_to_all | solution.py:194
  66.1 8.2 %collective-permute-start.6 = (bf16[128,1024]{1,0:T(8,128)(2,1)}, bf16[128,1024]{1,0:T(8,128)(2,1)S(1)}, u32[]{:S(2)}, u32[]{:S(2)}) collective-permute-start(bf16[128,1024]{1,0:T(8,128)(2,1)} %bitcast.97), channel_id=1, source_target_pairs={{128,0},{192,64},{1,128},{65,192},{129,1},{193,65},{0,129},{64,193... | collective-permute-start | bytes 786440 | tf_op jit(solution)/shard_map/ppermute | solution.py:32
  77.7 6.6 %collective-permute-done.6 = bf16[128,1024]{1,0:T(8,128)(2,1)S(1)} collective-permute-done((bf16[128,1024]{1,0:T(8,128)(2,1)}, bf16[128,1024]{1,0:T(8,128)(2,1)S(1)}, u32[]{:S(2)}, u32[]{:S(2)}) %collective-permute-start.6) | collective-permute-done | bytes 262176 | tf_op jit(solution)/shard_map/ppermute | solution.py:32
  86.5 7.2 %collective-permute-start.8 = (bf16[5,4,32,1024]{3,2,1,0:T(8,128)(2,1)}, bf16[5,4,32,1024]{3,2,1,0:T(8,128)(2,1)}, u32[]{:S(2)}, u32[]{:S(2)}) collective-permute-start(bf16[5,4,32,1024]{3,2,1,0:T(8,128)(2,1)} %constant_dynamic-update-slice_fusion.refs_0_), channel_id=1, source_target_pairs={{8,0},{0,8},{9,1},{1,9},{10,2},{2,10},{11,3},{3,11},{12,4},{4,12},... | collective-permute-start | bytes 3932168 | tf_op jit(solution)/shard_map/ppermute | solution.py:26
  93.8 3.2 %collective-permute-start.10 = (bf16[128,1024]{1,0:T(8,128)(2,1)S(1)}, bf16[128,1024]{1,0:T(8,128)(2,1)S(1)}, u32[]{:S(2)}, u32[]{:S(2)}) collective-permute-start(bf16[128,1024]{1,0:T(8,128)(2,1)S(1)} %bitcast.94), channel_id=1, source_target_pairs={{65,0},{129,64},{193,128},{0,192},{64,1},{128,65},{192,129},{1,193... | collective-permute-start | bytes 786440 | tf_op jit(solution)/shard_map/ppermute | solution.py:32
  97.0 4.4 %collective-permute-done.13.refs_7_ = bf16[4,2,128,256]{3,2,1,0:T(8,128)(2,1)S(1)} collective-permute-done((bf16[4,2,128,256]{3,2,1,0:T(8,128)(2,1)S(1)}, bf16[4,2,128,256]{3,2,1,0:T(8,128)(2,1)S(1)}, u32[]{:S(2)}, u32[]{:S(2)}) %collective-permute-start.13) | collective-permute-done | bytes 524320 | tf_op jit(solution)/shard_map/ppermute | solution.py:26
  102.3 3.6 %collective-permute-start.14 = (bf16[128,1024]{1,0:T(8,128)(2,1)S(1)}, bf16[128,1024]{1,0:T(8,128)(2,1)S(1)}, u32[]{:S(2)}, u32[]{:S(2)}) collective-permute-start(bf16[128,1024]{1,0:T(8,128)(2,1)S(1)} %bitcast.93), channel_id=1, source_target_pairs={{1,0},{65,64},{129,128},{193,192},{0,1},{64,65},{128,129},{192,193... | collective-permute-start | bytes 786440 | tf_op jit(solution)/shard_map/ppermute | solution.py:32
  105.8 9.3 %collective-permute-done.9 = bf16[128,1024]{1,0:T(8,128)(2,1)S(1)} collective-permute-done((bf16[128,1024]{1,0:T(8,128)(2,1)S(1)}, bf16[128,1024]{1,0:T(8,128)(2,1)S(1)}, u32[]{:S(2)}, u32[]{:S(2)}) %collective-permute-start.9) | collective-permute-done | bytes 262176 | tf_op jit(solution)/shard_map/ppermute | solution.py:32
  116.8 10.1 %collective-permute-done.14 = bf16[128,1024]{1,0:T(8,128)(2,1)S(1)} collective-permute-done((bf16[128,1024]{1,0:T(8,128)(2,1)S(1)}, bf16[128,1024]{1,0:T(8,128)(2,1)S(1)}, u32[]{:S(2)}, u32[]{:S(2)}) %collective-permute-start.14) | collective-permute-done | bytes 262176 | tf_op jit(solution)/shard_map/ppermute | solution.py:32
  131.1 5.5 %product.2 = (f32[512,256]{1,0:T(8,128)S(1)}, f32[2,272,256]{2,1,0:T(8,128)S(1)}, f32[2,272,256]{2,1,0:T(8,128)S(1)}, f32[2,272,256]{2,1,0:T(8,128)S(1)}) custom-call(s32[20]{0:T(128)S(1)} %stack.126.at, bf16[5,4,32,1024]{3,2,1,0:T(8,128)(2,1)} %constant_dynamic-update-slice_fusion.refs_0_, bf16[5,4,32,1024]{3,2,1,0:T(8,128)(2,1)} %collective-permute-done.8.refs_1_, ...), custom_call_target="tpu_custom_call" | custom-call | flops 2147483648 | bytes 8388608 | tf_op jit(solution)/shard_map/product/pallas_call | solution.py:144
  136.9 2.2 %collective-permute-start.17 = (f16[2,272,256]{2,1,0:T(8,128)(2,1)S(1)}, f16[2,272,256]{2,1,0:T(8,128)(2,1)S(1)}, u32[]{:S(2)}, u32[]{:S(2)}) collective-permute-start(f16[2,272,256]{2,1,0:T(8,128)(2,1)S(1)} %convert_element_type.57), channel_id=1, source_target_pairs={{32,0},{48,16},{0,32},{16,48},{33,1},{49,17},{1,33},{17,49},{34,2}... | collective-permute-start | bytes 835592 | tf_op jit(solution)/shard_map/ppermute | solution.py:26
  139.7 5.5 %product.3 = (f32[512,256]{1,0:T(8,128)S(1)}, f32[2,272,256]{2,1,0:T(8,128)S(1)}, f32[2,272,256]{2,1,0:T(8,128)S(1)}, f32[2,272,256]{2,1,0:T(8,128)S(1)}) custom-call(s32[20]{0:T(128)S(1)} %stack.126.at, bf16[5,4,32,1024]{3,2,1,0:T(8,128)(2,1)} %constant_dynamic-update-slice_fusion.refs_0_, bf16[5,4,32,1024]{3,2,1,0:T(8,128)(2,1)} %collective-permute-done.8.refs_1_, ...), custom_call_target="tpu_custom_call" | custom-call | flops 2147483648 | bytes 8388608 | tf_op jit(solution)/shard_map/product/pallas_call | solution.py:144
  147.9 2.1 %collective-permute-start.21 = (f16[2,272,256]{2,1,0:T(8,128)(2,1)S(1)}, f16[2,272,256]{2,1,0:T(8,128)(2,1)S(1)}, u32[]{:S(2)}, u32[]{:S(2)}) collective-permute-start(f16[2,272,256]{2,1,0:T(8,128)(2,1)S(1)} %convert_element_type.69), channel_id=1, source_target_pairs={{16,0},{32,16},{48,32},{0,48},{17,1},{33,17},{49,33},{1,49},{18,2}... | collective-permute-start | bytes 835592 | tf_op jit(solution)/shard_map/ppermute | solution.py:26
  152.3 11.9 %collective-permute-done.19 = f16[2,272,256]{2,1,0:T(8,128)(2,1)S(1)} collective-permute-done((f16[2,272,256]{2,1,0:T(8,128)(2,1)S(1)}, f16[2,272,256]{2,1,0:T(8,128)(2,1)S(1)}, u32[]{:S(2)}, u32[]{:S(2)}) %collective-permute-start.19) | collective-permute-done | bytes 278560 | tf_op jit(solution)/shard_map/ppermute | solution.py:26
  (84 shorter events, 33.6 us)
Async XLA Ops:
  3.5 26.6 %all-to-all-start = ((bf16[32,32,256]{2,1,0:T(8,128)(2,1)}), bf16[32,32,256]{2,1,0:T(8,128)(2,1)S(1)}, u32[]{:S(2)}, u32[]{:S(2)}) async-start(bf16[32,32,256]{2,1,0:T(8,128)(2,1)} %get-tuple-element.21), calls=%async_computation | async-start | bytes 1048576 | tf_op jit(solution)/shard_map/all_to_all | solution.py:180
  13.8 9.1 %collective-permute-start = (bf16[2,128,256]{2,1,0:T(8,128)(2,1)S(1)}, bf16[2,128,256]{2,1,0:T(8,128)(2,1)S(1)}, u32[]{:S(2)}, u32[]{:S(2)}) collective-permute-start(bf16[2,128,256]{2,1,0:T(8,128)(2,1)S(1)} %get-tuple-element.47), channel_id=1, source_target_pairs={{16,0},{32,16},{48,32},{0,48},{17,1},{33,17},{49,33},{1,49},{18,2}... | collective-permute-start | bytes 393224 | tf_op jit(solution)/shard_map/ppermute | solution.py:26
  16.5 8.3 %collective-permute-start.1 = (bf16[2,128,256]{2,1,0:T(8,128)(2,1)S(1)}, bf16[2,128,256]{2,1,0:T(8,128)(2,1)S(1)}, u32[]{:S(2)}, u32[]{:S(2)}) collective-permute-start(bf16[2,128,256]{2,1,0:T(8,128)(2,1)S(1)} %get-tuple-element.46), channel_id=1, source_target_pairs={{32,0},{48,16},{0,32},{16,48},{33,1},{49,17},{1,33},{17,49},{34,2}... | collective-permute-start | bytes 393224 | tf_op jit(solution)/shard_map/ppermute | solution.py:26
  17.1 11.8 %collective-permute-start.2 = (bf16[2,128,256]{2,1,0:T(8,128)(2,1)S(1)}, bf16[2,128,256]{2,1,0:T(8,128)(2,1)S(1)}, u32[]{:S(2)}, u32[]{:S(2)}) collective-permute-start(bf16[2,128,256]{2,1,0:T(8,128)(2,1)S(1)} %get-tuple-element.45), channel_id=1, source_target_pairs={{48,0},{0,16},{16,32},{32,48},{49,1},{1,17},{17,33},{33,49},{50,2}... | collective-permute-start | bytes 393224 | tf_op jit(solution)/shard_map/ppermute | solution.py:26
  32.8 13.9 %all-to-all-start.1 = ((bf16[4,2,32,1024]{3,2,1,0:T(8,128)(2,1)}), bf16[4,2,32,1024]{3,2,1,0:T(8,128)(2,1)S(1)}, u32[]{:S(2)}, u32[]{:S(2)}) async-start(bf16[4,2,32,1024]{3,2,1,0:T(8,128)(2,1)} %pick.1), calls=%async_computation.1 | async-start | bytes 1048576 | tf_op jit(solution)/shard_map/all_to_all | solution.py:198
  36.9 23.1 %collective-permute-start.5 = (bf16[4,2,128,256]{3,2,1,0:T(8,128)(2,1)S(1)}, bf16[4,2,128,256]{3,2,1,0:T(8,128)(2,1)S(1)}, u32[]{:S(2)}, u32[]{:S(2)}) collective-permute-start(bf16[4,2,128,256]{3,2,1,0:T(8,128)(2,1)S(1)} %pad_maximum_fusion.2.refs_4_), channel_id=1, source_target_pairs={{1,0},{0,1},{3,2},{2,3},{5,4},{4,5},{7,6},{6,7},{9,8},{8,9},{11,10... | collective-permute-start | bytes 1572872 | tf_op jit(solution)/shard_map/ppermute | solution.py:26
  47.8 27.2 %collective-permute-start.3 = (bf16[128,1024]{1,0:T(8,128)(2,1)}, bf16[128,1024]{1,0:T(8,128)(2,1)S(1)}, u32[]{:S(2)}, u32[]{:S(2)}) collective-permute-start(bf16[128,1024]{1,0:T(8,128)(2,1)} %bitcast.28), channel_id=1, source_target_pairs={{64,0},{128,64},{192,128},{1,192},{65,1},{129,65},{193,129},{0,193... | collective-permute-start | bytes 786440 | tf_op jit(solution)/shard_map/ppermute | solution.py:32
  50.1 26.2 %collective-permute-start.4 = (bf16[128,1024]{1,0:T(8,128)(2,1)}, bf16[128,1024]{1,0:T(8,128)(2,1)S(1)}, u32[]{:S(2)}, u32[]{:S(2)}) collective-permute-start(bf16[128,1024]{1,0:T(8,128)(2,1)} %bitcast.30), channel_id=1, source_target_pairs={{193,0},{0,64},{64,128},{128,192},{192,1},{1,65},{65,129},{129,193... | collective-permute-start | bytes 786440 | tf_op jit(solution)/shard_map/ppermute | solution.py:32
  50.1 43.8 %collective-permute-start.11 = (bf16[4,2,128,256]{3,2,1,0:T(8,128)(2,1)S(1)}, bf16[4,2,128,256]{3,2,1,0:T(8,128)(2,1)S(1)}, u32[]{:S(2)}, u32[]{:S(2)}) collective-permute-start(bf16[4,2,128,256]{3,2,1,0:T(8,128)(2,1)S(1)} %pad_maximum_fusion.2.refs_4_), channel_id=1, source_target_pairs={{2,0},{4,2},{6,4},{0,6},{3,1},{5,3},{7,5},{1,7},{10,8},{12,10},{14... | collective-permute-start | bytes 1572872 | tf_op jit(solution)/shard_map/ppermute | solution.py:26
  50.9 46.1 %collective-permute-start.12 = (bf16[4,2,128,256]{3,2,1,0:T(8,128)(2,1)S(1)}, bf16[4,2,128,256]{3,2,1,0:T(8,128)(2,1)S(1)}, u32[]{:S(2)}, u32[]{:S(2)}) collective-permute-start(bf16[4,2,128,256]{3,2,1,0:T(8,128)(2,1)S(1)} %pad_maximum_fusion.2.refs_4_), channel_id=1, source_target_pairs={{4,0},{6,2},{0,4},{2,6},{5,1},{7,3},{1,5},{3,7},{12,8},{14,10},{8,... | collective-permute-start | bytes 1572872 | tf_op jit(solution)/shard_map/ppermute | solution.py:26
  61.6 66.7 %all-to-all-start.2 = ((bf16[4,4,2,128,256]{4,3,2,1,0:T(8,128)(2,1)}), bf16[4,4,2,128,256]{4,3,2,1,0:T(8,128)(2,1)}, u32[]{:S(2)}, u32[]{:S(2)}) async-start(bf16[4,4,2,128,256]{4,3,2,1,0:T(8,128)(2,1)} %broadcast_in_dim.23), calls=%async_computation.2 | async-start | bytes 4194304 | tf_op jit(solution)/shard_map/all_to_all | solution.py:194
  66.1 18.3 %collective-permute-start.6 = (bf16[128,1024]{1,0:T(8,128)(2,1)}, bf16[128,1024]{1,0:T(8,128)(2,1)S(1)}, u32[]{:S(2)}, u32[]{:S(2)}) collective-permute-start(bf16[128,1024]{1,0:T(8,128)(2,1)} %bitcast.97), channel_id=1, source_target_pairs={{128,0},{192,64},{1,128},{65,192},{129,1},{193,65},{0,129},{64,193... | collective-permute-start | bytes 786440 | tf_op jit(solution)/shard_map/ppermute | solution.py:32
  75.0 26.5 %collective-permute-start.13 = (bf16[4,2,128,256]{3,2,1,0:T(8,128)(2,1)S(1)}, bf16[4,2,128,256]{3,2,1,0:T(8,128)(2,1)S(1)}, u32[]{:S(2)}, u32[]{:S(2)}) collective-permute-start(bf16[4,2,128,256]{3,2,1,0:T(8,128)(2,1)S(1)} %pad_maximum_fusion.2.refs_4_), channel_id=1, source_target_pairs={{6,0},{0,2},{2,4},{4,6},{7,1},{1,3},{3,5},{5,7},{14,8},{8,10},{10,... | collective-permute-start | bytes 1572872 | tf_op jit(solution)/shard_map/ppermute | solution.py:26
  76.3 9.5 %collective-permute-start.7 = (bf16[128,1024]{1,0:T(8,128)(2,1)}, bf16[128,1024]{1,0:T(8,128)(2,1)S(1)}, u32[]{:S(2)}, u32[]{:S(2)}) collective-permute-start(bf16[128,1024]{1,0:T(8,128)(2,1)} %bitcast.96), channel_id=1, source_target_pairs={{129,0},{193,64},{0,128},{64,192},{128,1},{192,65},{1,129},{65,193... | collective-permute-start | bytes 786440 | tf_op jit(solution)/shard_map/ppermute | solution.py:32
  86.5 43.6 %collective-permute-start.8 = (bf16[5,4,32,1024]{3,2,1,0:T(8,128)(2,1)}, bf16[5,4,32,1024]{3,2,1,0:T(8,128)(2,1)}, u32[]{:S(2)}, u32[]{:S(2)}) collective-permute-start(bf16[5,4,32,1024]{3,2,1,0:T(8,128)(2,1)} %constant_dynamic-update-slice_fusion.refs_0_), channel_id=1, source_target_pairs={{8,0},{0,8},{9,1},{1,9},{10,2},{2,10},{11,3},{3,11},{12,4},{4,12},... | collective-permute-start | bytes 3932168 | tf_op jit(solution)/shard_map/ppermute | solution.py:26
  93.8 21.3 %collective-permute-start.9 = (bf16[128,1024]{1,0:T(8,128)(2,1)S(1)}, bf16[128,1024]{1,0:T(8,128)(2,1)S(1)}, u32[]{:S(2)}, u32[]{:S(2)}) collective-permute-start(bf16[128,1024]{1,0:T(8,128)(2,1)S(1)} %bitcast.95), channel_id=1, source_target_pairs={{192,0},{1,64},{65,128},{129,192},{193,1},{0,65},{64,129},{128,193... | collective-permute-start | bytes 786440 | tf_op jit(solution)/shard_map/ppermute | solution.py:32
  93.8 23.0 %collective-permute-start.10 = (bf16[128,1024]{1,0:T(8,128)(2,1)S(1)}, bf16[128,1024]{1,0:T(8,128)(2,1)S(1)}, u32[]{:S(2)}, u32[]{:S(2)}) collective-permute-start(bf16[128,1024]{1,0:T(8,128)(2,1)S(1)} %bitcast.94), channel_id=1, source_target_pairs={{65,0},{129,64},{193,128},{0,192},{64,1},{128,65},{192,129},{1,193... | collective-permute-start | bytes 786440 | tf_op jit(solution)/shard_map/ppermute | solution.py:32
  102.3 24.6 %collective-permute-start.14 = (bf16[128,1024]{1,0:T(8,128)(2,1)S(1)}, bf16[128,1024]{1,0:T(8,128)(2,1)S(1)}, u32[]{:S(2)}, u32[]{:S(2)}) collective-permute-start(bf16[128,1024]{1,0:T(8,128)(2,1)S(1)} %bitcast.93), channel_id=1, source_target_pairs={{1,0},{65,64},{129,128},{193,192},{0,1},{64,65},{128,129},{192,193... | collective-permute-start | bytes 786440 | tf_op jit(solution)/shard_map/ppermute | solution.py:32
  136.7 11.2 %collective-permute-start.16 = (f16[2,272,256]{2,1,0:T(8,128)(2,1)S(1)}, f16[2,272,256]{2,1,0:T(8,128)(2,1)S(1)}, u32[]{:S(2)}, u32[]{:S(2)}) collective-permute-start(f16[2,272,256]{2,1,0:T(8,128)(2,1)S(1)} %convert_element_type.54), channel_id=1, source_target_pairs={{48,0},{0,16},{16,32},{32,48},{49,1},{1,17},{17,33},{33,49},{50,2}... | collective-permute-start | bytes 835592 | tf_op jit(solution)/shard_map/ppermute | solution.py:26
  136.9 14.5 %collective-permute-start.17 = (f16[2,272,256]{2,1,0:T(8,128)(2,1)S(1)}, f16[2,272,256]{2,1,0:T(8,128)(2,1)S(1)}, u32[]{:S(2)}, u32[]{:S(2)}) collective-permute-start(f16[2,272,256]{2,1,0:T(8,128)(2,1)S(1)} %convert_element_type.57), channel_id=1, source_target_pairs={{32,0},{48,16},{0,32},{16,48},{33,1},{49,17},{1,33},{17,49},{34,2}... | collective-permute-start | bytes 835592 | tf_op jit(solution)/shard_map/ppermute | solution.py:26
  139.1 13.2 %collective-permute-start.18 = (f16[2,272,256]{2,1,0:T(8,128)(2,1)S(1)}, f16[2,272,256]{2,1,0:T(8,128)(2,1)S(1)}, u32[]{:S(2)}, u32[]{:S(2)}) collective-permute-start(f16[2,272,256]{2,1,0:T(8,128)(2,1)S(1)} %convert_element_type.60), channel_id=1, source_target_pairs={{16,0},{32,16},{48,32},{0,48},{17,1},{33,17},{49,33},{1,49},{18,2}... | collective-permute-start | bytes 835592 | tf_op jit(solution)/shard_map/ppermute | solution.py:26
  145.3 18.9 %collective-permute-start.19 = (f16[2,272,256]{2,1,0:T(8,128)(2,1)S(1)}, f16[2,272,256]{2,1,0:T(8,128)(2,1)S(1)}, u32[]{:S(2)}, u32[]{:S(2)}) collective-permute-start(f16[2,272,256]{2,1,0:T(8,128)(2,1)S(1)} %convert_element_type.63), channel_id=1, source_target_pairs={{48,0},{0,16},{16,32},{32,48},{49,1},{1,17},{17,33},{33,49},{50,2}... | collective-permute-start | bytes 835592 | tf_op jit(solution)/shard_map/ppermute | solution.py:26
  146.3 17.9 %collective-permute-start.20 = (f16[2,272,256]{2,1,0:T(8,128)(2,1)S(1)}, f16[2,272,256]{2,1,0:T(8,128)(2,1)S(1)}, u32[]{:S(2)}, u32[]{:S(2)}) collective-permute-start(f16[2,272,256]{2,1,0:T(8,128)(2,1)S(1)} %convert_element_type.66), channel_id=1, source_target_pairs={{32,0},{48,16},{0,32},{16,48},{33,1},{49,17},{1,33},{17,49},{34,2}... | collective-permute-start | bytes 835592 | tf_op jit(solution)/shard_map/ppermute | solution.py:26
  147.9 16.4 %collective-permute-start.21 = (f16[2,272,256]{2,1,0:T(8,128)(2,1)S(1)}, f16[2,272,256]{2,1,0:T(8,128)(2,1)S(1)}, u32[]{:S(2)}, u32[]{:S(2)}) collective-permute-start(f16[2,272,256]{2,1,0:T(8,128)(2,1)S(1)} %convert_element_type.69), channel_id=1, source_target_pairs={{16,0},{32,16},{48,32},{0,48},{17,1},{33,17},{49,33},{1,49},{18,2}... | collective-permute-start | bytes 835592 | tf_op jit(solution)/shard_map/ppermute | solution.py:26
  (8 other events, 87.8 us)

commit v3 on v2

--- a/solution.py
+++ b/solution.py
@@ -43,7 +43,7 @@
     c = core[0]
     for i in range(rows // TILE):
         for j in range(width // TILE):
-            kept = tiles[i, j].astype(jnp.float32).astype(full.dtype)
+            kept = tiles[i, j].astype(full.dtype)
             cols = pl.ds(j * TILE, TILE)
             value = full[pl.ds(i * TILE, TILE), cols] * kept
             for k in range(TILE // piece):
@@ -67,7 +67,7 @@
         in_specs=[SMEM, SMEM, VMEM],
         out_specs=(VMEM, VMEM),
         name="mask",
-    )(core, tile_mask, interactions)
+    )(core, tile_mask.astype(jnp.float32), interactions)
 
 
 def pick_kernel(order, spread, out):
@@ -195,7 +195,7 @@
 
     stored = jnp.arange(panels, dtype=jnp.int32)
     order = jnp.sum(jnp.where(panel_of[None, :] == stored[:, None], stored[None, :], 0), 1).astype(jnp.int32)
-    mixed = lax.all_to_all(pick(order, tie(spread, mine)), "y", 0, 0, tiled=True)
+    mixed = lax.all_to_all(pick(order, spread), "y", 0, 0, tiled=True)
     flat = (-1, mixed.shape[-1])
 
     def side(h):
@@ -217,11 +217,11 @@
         return jnp.stack(out).astype(jnp.int32)
 
     held = {0: from_ring(0)}
-    for d in (1, -1):
+    for d in (-1, 1):
         held[d] = from_ring(d)
     for d in (2, -2):
         held[d] = from_ring(d, across)
-    for d in (3, -3):
+    for d in (-3, 3):
         held[d] = from_ring(d, across, held[1], held[-1])
     for d in (4,):
         held[d] = from_ring(d, held[1], held[-1], *near)

time: 166 us -> 166 us (level)
  starting transfers between devices: 63.5 us -> 61 us
  waiting for transfers between devices: 73.8 us -> 75.7 us
    all_to_all x1, waiting for transfers between devices: 1.13 us -> 11.7 us  [on_device(): spread = lax.all_to_all(blocks, BLK, 0, 0, tiled=True)]
    ppermute x7, waiting for transfers between devices: 28.4 us -> 20.7 us  [along(): lax.ppermute(a, LINE, [(index[(i + by) % n], index[i]) for i in range(n)])]
    ppermute x7, starting transfers between devices: 17.3 us -> 14 us  [along(): lax.ppermute(a, LINE, [(index[(i + by) % n], index[i]) for i in range(n)])]
  transfers between devices with their start and end apart: 25 -> 25, of which waited for: 16 -> 13; matrix products, arithmetic and copies ran while one was open for 5% -> 5% of each run, Pallas kernels for 3% -> 4%
where the time goes in v3:
time: 166 us; the launch traced here: 165 us
  waiting for transfers between devices  75.7 us (46%)
  starting transfers between devices  61 us (37%)
  Pallas kernels  15.1 us (9%)
  local copies, waits for them, and re-layouts  9.88 us (6%)
  other arithmetic  3.29 us (2%)
    ppermute x15, waiting for transfers between devices, shift(): return lax.ppermute(a, axis, [((i + by) % n, i) for i in range(n)])  38 us
    ppermute x15, starting transfers between devices, shift(): return lax.ppermute(a, axis, [((i + by) % n, i) for i in range(n)])  28.2 us
    ppermute x7, waiting for transfers between devices, along(): lax.ppermute(a, LINE, [(index[(i + by) % n], index[i]) for i in range(n)])  20.7 us
    ppermute x7, starting transfers between devices, along(): lax.ppermute(a, LINE, [(index[(i + by) % n], index[i]) for i in range(n)])  14 us
    all_to_all x1, waiting for transfers between devices, on_device(): spread = lax.all_to_all(blocks, BLK, 0, 0, tiled=True)  11.7 us
    pallas_call x2, Pallas kernels, product(): pl.pallas_call(functools.partial(product_kernel, groups, len(near)), out_...  11 us
    all_to_all x1, starting transfers between devices, on_device(): spread = lax.all_to_all(blocks, BLK, 0, 0, tiled=True)  10.1 us
    unnamed x25, local copies, waits for them, and re-layouts  6.29 us
  transfers between devices with their start and end apart: 25, of which 13 were waited for; matrix products, arithmetic and copies ran while one was open for 5% of the time, Pallas kernels for 4%

profile of v3, /device:TPU:1, one launch (start us, length us, event | category | flops | bytes accessed | tf_op | source)
XLA Modules:
  0.0 165.4 jit_solution(11614795030550100833)
XLA Ops:
  1.4 2.2 %mask.1 = (bf16[32,32,256]{2,1,0:T(8,128)(2,1)}, bf16[4,2,128,256]{3,2,1,0:T(8,128)(2,1)}) custom-call(s32[1]{0:T(128)} %bitcast.20.core, f32[8,2]{1,0:T(8,128)} %convert_element_type.57.tiles, bf16[1024,256]{1,0:T(8,128)(2,1)} %full.1), custom_call_target="tpu_custom_call" | custom-call | tf_op jit(solution)/shard_map/mask/pallas_call | solution.py:61
  3.5 10.1 %all-to-all-start = ((bf16[32,32,256]{2,1,0:T(8,128)(2,1)}), bf16[32,32,256]{2,1,0:T(8,128)(2,1)S(1)}, u32[]{:S(2)}, u32[]{:S(2)}) async-start(bf16[32,32,256]{2,1,0:T(8,128)(2,1)} %get-tuple-element.20), calls=%async_computation | async-start | bytes 1048576 | tf_op jit(solution)/shard_map/all_to_all | solution.py:180
  13.8 2.7 %collective-permute-start.2 = (bf16[2,128,256]{2,1,0:T(8,128)(2,1)S(1)}, bf16[2,128,256]{2,1,0:T(8,128)(2,1)S(1)}, u32[]{:S(2)}, u32[]{:S(2)}) collective-permute-start(bf16[2,128,256]{2,1,0:T(8,128)(2,1)S(1)} %get-tuple-element.45), channel_id=1, source_target_pairs={{16,0},{32,16},{48,32},{0,48},{17,1},{33,17},{49,33},{1,49},{18,2}... | collective-permute-start | bytes 393224 | tf_op jit(solution)/shard_map/ppermute | solution.py:26
  18.3 11.7 %all-to-all-done.spread = bf16[32,32,256]{2,1,0:T(8,128)(2,1)S(1)} async-done(((bf16[32,32,256]{2,1,0:T(8,128)(2,1)}), bf16[32,32,256]{2,1,0:T(8,128)(2,1)S(1)}, u32[]{:S(2)}, u32[]{:S(2)}) %all-to-all-start) | async-done | bytes 524320 | tf_op jit(solution)/shard_map/all_to_all | solution.py:180
  32.8 4.2 %all-to-all-start.1 = ((bf16[4,2,32,1024]{3,2,1,0:T(8,128)(2,1)}), bf16[4,2,32,1024]{3,2,1,0:T(8,128)(2,1)S(1)}, u32[]{:S(2)}, u32[]{:S(2)}) async-start(bf16[4,2,32,1024]{3,2,1,0:T(8,128)(2,1)} %pick.1), calls=%async_computation.1 | async-start | bytes 1048576 | tf_op jit(solution)/shard_map/all_to_all | solution.py:198
  37.0 4.3 %collective-permute-start.5 = (bf16[4,2,128,256]{3,2,1,0:T(8,128)(2,1)S(1)}, bf16[4,2,128,256]{3,2,1,0:T(8,128)(2,1)S(1)}, u32[]{:S(2)}, u32[]{:S(2)}) collective-permute-start(bf16[4,2,128,256]{3,2,1,0:T(8,128)(2,1)S(1)} %pad_maximum_fusion.2.refs_4_), channel_id=1, source_target_pairs={{1,0},{0,1},{3,2},{2,3},{5,4},{4,5},{7,6},{6,7},{9,8},{8,9},{11,10... | collective-permute-start | bytes 1572872 | tf_op jit(solution)/shard_map/ppermute | solution.py:26
  41.3 5.3 %all-to-all-done.1 = bf16[4,2,32,1024]{3,2,1,0:T(8,128)(2,1)S(1)} async-done(((bf16[4,2,32,1024]{3,2,1,0:T(8,128)(2,1)}), bf16[4,2,32,1024]{3,2,1,0:T(8,128)(2,1)S(1)}, u32[]{:S(2)}, u32[]{:S(2)}) %all-to-all-start.1) | async-done | bytes 524320 | tf_op jit(solution)/shard_map/all_to_all | solution.py:198
  47.8 2.7 %collective-permute-start = (bf16[128,1024]{1,0:T(8,128)(2,1)}, bf16[128,1024]{1,0:T(8,128)(2,1)S(1)}, u32[]{:S(2)}, u32[]{:S(2)}) collective-permute-start(bf16[128,1024]{1,0:T(8,128)(2,1)} %bitcast.22), channel_id=1, source_target_pairs={{64,0},{128,64},{192,128},{1,192},{65,1},{129,65},{193,129},{0,193... | collective-permute-start | bytes 786440 | tf_op jit(solution)/shard_map/ppermute | solution.py:32
  52.6 12.5 %collective-permute-done.5 = bf16[4,2,128,256]{3,2,1,0:T(8,128)(2,1)S(1)} collective-permute-done((bf16[4,2,128,256]{3,2,1,0:T(8,128)(2,1)S(1)}, bf16[4,2,128,256]{3,2,1,0:T(8,128)(2,1)S(1)}, u32[]{:S(2)}, u32[]{:S(2)}) %collective-permute-start.5) | collective-permute-done | bytes 524320 | tf_op jit(solution)/shard_map/ppermute | solution.py:26
  66.6 4.4 %all-to-all-start.2 = ((bf16[4,4,2,128,256]{4,3,2,1,0:T(8,128)(2,1)}), bf16[4,4,2,128,256]{4,3,2,1,0:T(8,128)(2,1)}, u32[]{:S(2)}, u32[]{:S(2)}) async-start(bf16[4,4,2,128,256]{4,3,2,1,0:T(8,128)(2,1)} %broadcast_in_dim.23), calls=%async_computation.2 | async-start | bytes 4194304 | tf_op jit(solution)/shard_map/all_to_all | solution.py:194
  73.2 2.4 %collective-permute-start.7 = (bf16[128,1024]{1,0:T(8,128)(2,1)}, bf16[128,1024]{1,0:T(8,128)(2,1)S(1)}, u32[]{:S(2)}, u32[]{:S(2)}) collective-permute-start(bf16[128,1024]{1,0:T(8,128)(2,1)} %bitcast.96), channel_id=1, source_target_pairs={{129,0},{193,64},{0,128},{64,192},{128,1},{192,65},{1,129},{65,193... | collective-permute-start | bytes 786440 | tf_op jit(solution)/shard_map/ppermute | solution.py:32
  77.0 8.3 %collective-permute-done.6 = bf16[128,1024]{1,0:T(8,128)(2,1)S(1)} collective-permute-done((bf16[128,1024]{1,0:T(8,128)(2,1)}, bf16[128,1024]{1,0:T(8,128)(2,1)S(1)}, u32[]{:S(2)}, u32[]{:S(2)}) %collective-permute-start.6) | collective-permute-done | bytes 262176 | tf_op jit(solution)/shard_map/ppermute | solution.py:32
  86.7 7.3 %collective-permute-start.8 = (bf16[5,4,32,1024]{3,2,1,0:T(8,128)(2,1)}, bf16[5,4,32,1024]{3,2,1,0:T(8,128)(2,1)}, u32[]{:S(2)}, u32[]{:S(2)}) collective-permute-start(bf16[5,4,32,1024]{3,2,1,0:T(8,128)(2,1)} %constant_dynamic-update-slice_fusion.refs_0_), channel_id=1, source_target_pairs={{8,0},{0,8},{9,1},{1,9},{10,2},{2,10},{11,3},{3,11},{12,4},{4,12},... | collective-permute-start | bytes 3932168 | tf_op jit(solution)/shard_map/ppermute | solution.py:26
  94.1 3.3 %collective-permute-start.10 = (bf16[128,1024]{1,0:T(8,128)(2,1)S(1)}, bf16[128,1024]{1,0:T(8,128)(2,1)S(1)}, u32[]{:S(2)}, u32[]{:S(2)}) collective-permute-start(bf16[128,1024]{1,0:T(8,128)(2,1)S(1)} %bitcast.94), channel_id=1, source_target_pairs={{65,0},{129,64},{193,128},{0,192},{64,1},{128,65},{192,129},{1,193... | collective-permute-start | bytes 786440 | tf_op jit(solution)/shard_map/ppermute | solution.py:32
  97.4 9.6 %collective-permute-done.13.refs_7_ = bf16[4,2,128,256]{3,2,1,0:T(8,128)(2,1)S(1)} collective-permute-done((bf16[4,2,128,256]{3,2,1,0:T(8,128)(2,1)S(1)}, bf16[4,2,128,256]{3,2,1,0:T(8,128)(2,1)S(1)}, u32[]{:S(2)}, u32[]{:S(2)}) %collective-permute-start.13) | collective-permute-done | bytes 524320 | tf_op jit(solution)/shard_map/ppermute | solution.py:26
  107.8 5.6 %collective-permute-start.14 = (bf16[128,1024]{1,0:T(8,128)(2,1)S(1)}, bf16[128,1024]{1,0:T(8,128)(2,1)S(1)}, u32[]{:S(2)}, u32[]{:S(2)}) collective-permute-start(bf16[128,1024]{1,0:T(8,128)(2,1)S(1)} %bitcast.93), channel_id=1, source_target_pairs={{1,0},{65,64},{129,128},{193,192},{0,1},{64,65},{128,129},{192,193... | collective-permute-start | bytes 786440 | tf_op jit(solution)/shard_map/ppermute | solution.py:32
  114.1 3.1 %collective-permute-done.10 = bf16[128,1024]{1,0:T(8,128)(2,1)S(1)} collective-permute-done((bf16[128,1024]{1,0:T(8,128)(2,1)S(1)}, bf16[128,1024]{1,0:T(8,128)(2,1)S(1)}, u32[]{:S(2)}, u32[]{:S(2)}) %collective-permute-start.10) | collective-permute-done | bytes 262176 | tf_op jit(solution)/shard_map/ppermute | solution.py:32
  117.2 8.5 %collective-permute-done.14 = bf16[128,1024]{1,0:T(8,128)(2,1)S(1)} collective-permute-done((bf16[128,1024]{1,0:T(8,128)(2,1)S(1)}, bf16[128,1024]{1,0:T(8,128)(2,1)S(1)}, u32[]{:S(2)}, u32[]{:S(2)}) %collective-permute-start.14) | collective-permute-done | bytes 262176 | tf_op jit(solution)/shard_map/ppermute | solution.py:32
  130.6 5.5 %product.2 = (f32[512,256]{1,0:T(8,128)S(1)}, f32[2,272,256]{2,1,0:T(8,128)S(1)}, f32[2,272,256]{2,1,0:T(8,128)S(1)}, f32[2,272,256]{2,1,0:T(8,128)S(1)}) custom-call(s32[20]{0:T(128)S(1)} %stack.126.at, bf16[5,4,32,1024]{3,2,1,0:T(8,128)(2,1)} %constant_dynamic-update-slice_fusion.refs_0_, bf16[5,4,32,1024]{3,2,1,0:T(8,128)(2,1)} %collective-permute-done.8.refs_1_, ...), custom_call_target="tpu_custom_call" | custom-call | flops 2147483648 | bytes 8388608 | tf_op jit(solution)/shard_map/product/pallas_call | solution.py:144
  136.3 3.2 %collective-permute-start.17 = (f16[2,272,256]{2,1,0:T(8,128)(2,1)S(1)}, f16[2,272,256]{2,1,0:T(8,128)(2,1)S(1)}, u32[]{:S(2)}, u32[]{:S(2)}) collective-permute-start(f16[2,272,256]{2,1,0:T(8,128)(2,1)S(1)} %convert_element_type.61), channel_id=1, source_target_pairs={{32,0},{48,16},{0,32},{16,48},{33,1},{49,17},{1,33},{17,49},{34,2}... | collective-permute-start | bytes 835592 | tf_op jit(solution)/shard_map/ppermute | solution.py:26
  139.6 5.5 %product.3 = (f32[512,256]{1,0:T(8,128)S(1)}, f32[2,272,256]{2,1,0:T(8,128)S(1)}, f32[2,272,256]{2,1,0:T(8,128)S(1)}, f32[2,272,256]{2,1,0:T(8,128)S(1)}) custom-call(s32[20]{0:T(128)S(1)} %stack.126.at, bf16[5,4,32,1024]{3,2,1,0:T(8,128)(2,1)} %constant_dynamic-update-slice_fusion.refs_0_, bf16[5,4,32,1024]{3,2,1,0:T(8,128)(2,1)} %collective-permute-done.8.refs_1_, ...), custom_call_target="tpu_custom_call" | custom-call | flops 2147483648 | bytes 8388608 | tf_op jit(solution)/shard_map/product/pallas_call | solution.py:144
  149.5 2.2 %collective-permute-done.17 = f16[2,272,256]{2,1,0:T(8,128)(2,1)S(1)} collective-permute-done((f16[2,272,256]{2,1,0:T(8,128)(2,1)S(1)}, f16[2,272,256]{2,1,0:T(8,128)(2,1)S(1)}, u32[]{:S(2)}, u32[]{:S(2)}) %collective-permute-start.17) | collective-permute-done | bytes 278560 | tf_op jit(solution)/shard_map/ppermute | solution.py:26
  152.2 6.9 %collective-permute-done.19 = f16[2,272,256]{2,1,0:T(8,128)(2,1)S(1)} collective-permute-done((f16[2,272,256]{2,1,0:T(8,128)(2,1)S(1)}, f16[2,272,256]{2,1,0:T(8,128)(2,1)S(1)}, u32[]{:S(2)}, u32[]{:S(2)}) %collective-permute-start.19) | collective-permute-done | bytes 278560 | tf_op jit(solution)/shard_map/ppermute | solution.py:26
  159.1 4.6 %collective-permute-done.20 = f16[2,272,256]{2,1,0:T(8,128)(2,1)S(1)} collective-permute-done((f16[2,272,256]{2,1,0:T(8,128)(2,1)S(1)}, f16[2,272,256]{2,1,0:T(8,128)(2,1)S(1)}, u32[]{:S(2)}, u32[]{:S(2)}) %collective-permute-start.20) | collective-permute-done | bytes 278560 | tf_op jit(solution)/shard_map/ppermute | solution.py:26
  (85 shorter events, 28.8 us)
Async XLA Ops:
  3.5 26.6 %all-to-all-start = ((bf16[32,32,256]{2,1,0:T(8,128)(2,1)}), bf16[32,32,256]{2,1,0:T(8,128)(2,1)S(1)}, u32[]{:S(2)}, u32[]{:S(2)}) async-start(bf16[32,32,256]{2,1,0:T(8,128)(2,1)} %get-tuple-element.20), calls=%async_computation | async-start | bytes 1048576 | tf_op jit(solution)/shard_map/all_to_all | solution.py:180
  13.8 23.1 %collective-permute-start.2 = (bf16[2,128,256]{2,1,0:T(8,128)(2,1)S(1)}, bf16[2,128,256]{2,1,0:T(8,128)(2,1)S(1)}, u32[]{:S(2)}, u32[]{:S(2)}) collective-permute-start(bf16[2,128,256]{2,1,0:T(8,128)(2,1)S(1)} %get-tuple-element.45), channel_id=1, source_target_pairs={{16,0},{32,16},{48,32},{0,48},{17,1},{33,17},{49,33},{1,49},{18,2}... | collective-permute-start | bytes 393224 | tf_op jit(solution)/shard_map/ppermute | solution.py:26
  16.5 20.5 %collective-permute-start.3 = (bf16[2,128,256]{2,1,0:T(8,128)(2,1)S(1)}, bf16[2,128,256]{2,1,0:T(8,128)(2,1)S(1)}, u32[]{:S(2)}, u32[]{:S(2)}) collective-permute-start(bf16[2,128,256]{2,1,0:T(8,128)(2,1)S(1)} %get-tuple-element.44), channel_id=1, source_target_pairs={{32,0},{48,16},{0,32},{16,48},{33,1},{49,17},{1,33},{17,49},{34,2}... | collective-permute-start | bytes 393224 | tf_op jit(solution)/shard_map/ppermute | solution.py:26
  17.1 19.9 %collective-permute-start.4 = (bf16[2,128,256]{2,1,0:T(8,128)(2,1)S(1)}, bf16[2,128,256]{2,1,0:T(8,128)(2,1)S(1)}, u32[]{:S(2)}, u32[]{:S(2)}) collective-permute-start(bf16[2,128,256]{2,1,0:T(8,128)(2,1)S(1)} %get-tuple-element.43), channel_id=1, source_target_pairs={{48,0},{0,16},{16,32},{32,48},{49,1},{1,17},{17,33},{33,49},{50,2}... | collective-permute-start | bytes 393224 | tf_op jit(solution)/shard_map/ppermute | solution.py:26
  32.8 13.9 %all-to-all-start.1 = ((bf16[4,2,32,1024]{3,2,1,0:T(8,128)(2,1)}), bf16[4,2,32,1024]{3,2,1,0:T(8,128)(2,1)S(1)}, u32[]{:S(2)}, u32[]{:S(2)}) async-start(bf16[4,2,32,1024]{3,2,1,0:T(8,128)(2,1)} %pick.1), calls=%async_computation.1 | async-start | bytes 1048576 | tf_op jit(solution)/shard_map/all_to_all | solution.py:198
  37.0 28.0 %collective-permute-start.5 = (bf16[4,2,128,256]{3,2,1,0:T(8,128)(2,1)S(1)}, bf16[4,2,128,256]{3,2,1,0:T(8,128)(2,1)S(1)}, u32[]{:S(2)}, u32[]{:S(2)}) collective-permute-start(bf16[4,2,128,256]{3,2,1,0:T(8,128)(2,1)S(1)} %pad_maximum_fusion.2.refs_4_), channel_id=1, source_target_pairs={{1,0},{0,1},{3,2},{2,3},{5,4},{4,5},{7,6},{6,7},{9,8},{8,9},{11,10... | collective-permute-start | bytes 1572872 | tf_op jit(solution)/shard_map/ppermute | solution.py:26
  47.8 24.1 %collective-permute-start = (bf16[128,1024]{1,0:T(8,128)(2,1)}, bf16[128,1024]{1,0:T(8,128)(2,1)S(1)}, u32[]{:S(2)}, u32[]{:S(2)}) collective-permute-start(bf16[128,1024]{1,0:T(8,128)(2,1)} %bitcast.22), channel_id=1, source_target_pairs={{64,0},{128,64},{192,128},{1,192},{65,1},{129,65},{193,129},{0,193... | collective-permute-start | bytes 786440 | tf_op jit(solution)/shard_map/ppermute | solution.py:32
  50.5 22.7 %collective-permute-start.1 = (bf16[128,1024]{1,0:T(8,128)(2,1)}, bf16[128,1024]{1,0:T(8,128)(2,1)S(1)}, u32[]{:S(2)}, u32[]{:S(2)}) collective-permute-start(bf16[128,1024]{1,0:T(8,128)(2,1)} %bitcast.24), channel_id=1, source_target_pairs={{193,0},{0,64},{64,128},{128,192},{192,1},{1,65},{65,129},{129,193... | collective-permute-start | bytes 786440 | tf_op jit(solution)/shard_map/ppermute | solution.py:32
  50.5 43.6 %collective-permute-start.11 = (bf16[4,2,128,256]{3,2,1,0:T(8,128)(2,1)S(1)}, bf16[4,2,128,256]{3,2,1,0:T(8,128)(2,1)S(1)}, u32[]{:S(2)}, u32[]{:S(2)}) collective-permute-start(bf16[4,2,128,256]{3,2,1,0:T(8,128)(2,1)S(1)} %pad_maximum_fusion.2.refs_4_), channel_id=1, source_target_pairs={{2,0},{4,2},{6,4},{0,6},{3,1},{5,3},{7,5},{1,7},{10,8},{12,10},{14... | collective-permute-start | bytes 1572872 | tf_op jit(solution)/shard_map/ppermute | solution.py:26
  51.4 46.0 %collective-permute-start.12 = (bf16[4,2,128,256]{3,2,1,0:T(8,128)(2,1)S(1)}, bf16[4,2,128,256]{3,2,1,0:T(8,128)(2,1)S(1)}, u32[]{:S(2)}, u32[]{:S(2)}) collective-permute-start(bf16[4,2,128,256]{3,2,1,0:T(8,128)(2,1)S(1)} %pad_maximum_fusion.2.refs_4_), channel_id=1, source_target_pairs={{4,0},{6,2},{0,4},{2,6},{5,1},{7,3},{1,5},{3,7},{12,8},{14,10},{8,... | collective-permute-start | bytes 1572872 | tf_op jit(solution)/shard_map/ppermute | solution.py:26
  66.6 61.1 %all-to-all-start.2 = ((bf16[4,4,2,128,256]{4,3,2,1,0:T(8,128)(2,1)}), bf16[4,4,2,128,256]{4,3,2,1,0:T(8,128)(2,1)}, u32[]{:S(2)}, u32[]{:S(2)}) async-start(bf16[4,4,2,128,256]{4,3,2,1,0:T(8,128)(2,1)} %broadcast_in_dim.23), calls=%async_computation.2 | async-start | bytes 4194304 | tf_op jit(solution)/shard_map/all_to_all | solution.py:194
  71.1 14.2 %collective-permute-start.6 = (bf16[128,1024]{1,0:T(8,128)(2,1)}, bf16[128,1024]{1,0:T(8,128)(2,1)S(1)}, u32[]{:S(2)}, u32[]{:S(2)}) collective-permute-start(bf16[128,1024]{1,0:T(8,128)(2,1)} %bitcast.97), channel_id=1, source_target_pairs={{128,0},{192,64},{1,128},{65,192},{129,1},{193,65},{0,129},{64,193... | collective-permute-start | bytes 786440 | tf_op jit(solution)/shard_map/ppermute | solution.py:32
  71.9 35.1 %collective-permute-start.13 = (bf16[4,2,128,256]{3,2,1,0:T(8,128)(2,1)S(1)}, bf16[4,2,128,256]{3,2,1,0:T(8,128)(2,1)S(1)}, u32[]{:S(2)}, u32[]{:S(2)}) collective-permute-start(bf16[4,2,128,256]{3,2,1,0:T(8,128)(2,1)S(1)} %pad_maximum_fusion.2.refs_4_), channel_id=1, source_target_pairs={{6,0},{0,2},{2,4},{4,6},{7,1},{1,3},{3,5},{5,7},{14,8},{8,10},{10,... | collective-permute-start | bytes 1572872 | tf_op jit(solution)/shard_map/ppermute | solution.py:26
  73.2 12.8 %collective-permute-start.7 = (bf16[128,1024]{1,0:T(8,128)(2,1)}, bf16[128,1024]{1,0:T(8,128)(2,1)S(1)}, u32[]{:S(2)}, u32[]{:S(2)}) collective-permute-start(bf16[128,1024]{1,0:T(8,128)(2,1)} %bitcast.96), channel_id=1, source_target_pairs={{129,0},{193,64},{0,128},{64,192},{128,1},{192,65},{1,129},{65,193... | collective-permute-start | bytes 786440 | tf_op jit(solution)/shard_map/ppermute | solution.py:32
  86.7 42.8 %collective-permute-start.8 = (bf16[5,4,32,1024]{3,2,1,0:T(8,128)(2,1)}, bf16[5,4,32,1024]{3,2,1,0:T(8,128)(2,1)}, u32[]{:S(2)}, u32[]{:S(2)}) collective-permute-start(bf16[5,4,32,1024]{3,2,1,0:T(8,128)(2,1)} %constant_dynamic-update-slice_fusion.refs_0_), channel_id=1, source_target_pairs={{8,0},{0,8},{9,1},{1,9},{10,2},{2,10},{11,3},{3,11},{12,4},{4,12},... | collective-permute-start | bytes 3932168 | tf_op jit(solution)/shard_map/ppermute | solution.py:26
  94.1 20.1 %collective-permute-start.9 = (bf16[128,1024]{1,0:T(8,128)(2,1)S(1)}, bf16[128,1024]{1,0:T(8,128)(2,1)S(1)}, u32[]{:S(2)}, u32[]{:S(2)}) collective-permute-start(bf16[128,1024]{1,0:T(8,128)(2,1)S(1)} %bitcast.95), channel_id=1, source_target_pairs={{192,0},{1,64},{65,128},{129,192},{193,1},{0,65},{64,129},{128,193... | collective-permute-start | bytes 786440 | tf_op jit(solution)/shard_map/ppermute | solution.py:32
  94.1 23.1 %collective-permute-start.10 = (bf16[128,1024]{1,0:T(8,128)(2,1)S(1)}, bf16[128,1024]{1,0:T(8,128)(2,1)S(1)}, u32[]{:S(2)}, u32[]{:S(2)}) collective-permute-start(bf16[128,1024]{1,0:T(8,128)(2,1)S(1)} %bitcast.94), channel_id=1, source_target_pairs={{65,0},{129,64},{193,128},{0,192},{64,1},{128,65},{192,129},{1,193... | collective-permute-start | bytes 786440 | tf_op jit(solution)/shard_map/ppermute | solution.py:32
  107.8 18.0 %collective-permute-start.14 = (bf16[128,1024]{1,0:T(8,128)(2,1)S(1)}, bf16[128,1024]{1,0:T(8,128)(2,1)S(1)}, u32[]{:S(2)}, u32[]{:S(2)}) collective-permute-start(bf16[128,1024]{1,0:T(8,128)(2,1)S(1)} %bitcast.93), channel_id=1, source_target_pairs={{1,0},{65,64},{129,128},{193,192},{0,1},{64,65},{128,129},{192,193... | collective-permute-start | bytes 786440 | tf_op jit(solution)/shard_map/ppermute | solution.py:32
  136.2 11.2 %collective-permute-start.16 = (f16[2,272,256]{2,1,0:T(8,128)(2,1)S(1)}, f16[2,272,256]{2,1,0:T(8,128)(2,1)S(1)}, u32[]{:S(2)}, u32[]{:S(2)}) collective-permute-start(f16[2,272,256]{2,1,0:T(8,128)(2,1)S(1)} %convert_element_type.58), channel_id=1, source_target_pairs={{48,0},{0,16},{16,32},{32,48},{49,1},{1,17},{17,33},{33,49},{50,2}... | collective-permute-start | bytes 835592 | tf_op jit(solution)/shard_map/ppermute | solution.py:26
  136.3 15.5 %collective-permute-start.17 = (f16[2,272,256]{2,1,0:T(8,128)(2,1)S(1)}, f16[2,272,256]{2,1,0:T(8,128)(2,1)S(1)}, u32[]{:S(2)}, u32[]{:S(2)}) collective-permute-start(f16[2,272,256]{2,1,0:T(8,128)(2,1)S(1)} %convert_element_type.61), channel_id=1, source_target_pairs={{32,0},{48,16},{0,32},{16,48},{33,1},{49,17},{1,33},{17,49},{34,2}... | collective-permute-start | bytes 835592 | tf_op jit(solution)/shard_map/ppermute | solution.py:26
  139.5 12.6 %collective-permute-start.18 = (f16[2,272,256]{2,1,0:T(8,128)(2,1)S(1)}, f16[2,272,256]{2,1,0:T(8,128)(2,1)S(1)}, u32[]{:S(2)}, u32[]{:S(2)}) collective-permute-start(f16[2,272,256]{2,1,0:T(8,128)(2,1)S(1)} %convert_element_type.64), channel_id=1, source_target_pairs={{16,0},{32,16},{48,32},{0,48},{17,1},{33,17},{49,33},{1,49},{18,2}... | collective-permute-start | bytes 835592 | tf_op jit(solution)/shard_map/ppermute | solution.py:26
  145.2 13.9 %collective-permute-start.19 = (f16[2,272,256]{2,1,0:T(8,128)(2,1)S(1)}, f16[2,272,256]{2,1,0:T(8,128)(2,1)S(1)}, u32[]{:S(2)}, u32[]{:S(2)}) collective-permute-start(f16[2,272,256]{2,1,0:T(8,128)(2,1)S(1)} %convert_element_type.67), channel_id=1, source_target_pairs={{48,0},{0,16},{16,32},{32,48},{49,1},{1,17},{17,33},{33,49},{50,2}... | collective-permute-start | bytes 835592 | tf_op jit(solution)/shard_map/ppermute | solution.py:26
  146.8 16.9 %collective-permute-start.20 = (f16[2,272,256]{2,1,0:T(8,128)(2,1)S(1)}, f16[2,272,256]{2,1,0:T(8,128)(2,1)S(1)}, u32[]{:S(2)}, u32[]{:S(2)}) collective-permute-start(f16[2,272,256]{2,1,0:T(8,128)(2,1)S(1)} %convert_element_type.70), channel_id=1, source_target_pairs={{32,0},{48,16},{0,32},{16,48},{33,1},{49,17},{1,33},{17,49},{34,2}... | collective-permute-start | bytes 835592 | tf_op jit(solution)/shard_map/ppermute | solution.py:26
  147.4 16.4 %collective-permute-start.21 = (f16[2,272,256]{2,1,0:T(8,128)(2,1)S(1)}, f16[2,272,256]{2,1,0:T(8,128)(2,1)S(1)}, u32[]{:S(2)}, u32[]{:S(2)}) collective-permute-start(f16[2,272,256]{2,1,0:T(8,128)(2,1)S(1)} %convert_element_type.73), channel_id=1, source_target_pairs={{16,0},{32,16},{48,32},{0,48},{17,1},{33,17},{49,33},{1,49},{18,2}... | collective-permute-start | bytes 835592 | tf_op jit(solution)/shard_map/ppermute | solution.py:26
  (8 other events, 78.9 us)

commit v4 on v3

--- a/solution.py
+++ b/solution.py
@@ -232,7 +232,7 @@
     done = []
     for lo, size in ROWS:
         total, *sent = product(where(), sides, near, away, lo, size)
-        for dx in range(1, nx):
+        for dx in (2, 1, 3):
             total = total + opened(shift(sent[dx - 1].astype(jnp.float16), "x", -dx))
         done.append(total)
     return jnp.concatenate(done, 0)

time: 166 us -> 166 us (level)
  transfers between devices with their start and end apart: 25 -> 25, of which waited for: 13 -> 12; matrix products, arithmetic and copies ran while one was open for 5% -> 5% of each run, Pallas kernels for 4% -> 4%
where the time goes in v4:
time: 166 us
  waiting for transfers between devices  75.9 us (46%)
  starting transfers between devices  61 us (37%)
  Pallas kernels  15.1 us (9%)
  local copies, waits for them, and re-layouts  9.88 us (6%)
  other arithmetic  3.29 us (2%)
    ppermute x15, waiting for transfers between devices, shift(): return lax.ppermute(a, axis, [((i + by) % n, i) for i in range(n)])  38.2 us
    ppermute x15, starting transfers between devices, shift(): return lax.ppermute(a, axis, [((i + by) % n, i) for i in range(n)])  28.2 us
    ppermute x7, waiting for transfers between devices, along(): lax.ppermute(a, LINE, [(index[(i + by) % n], index[i]) for i in range(n)])  20.7 us
    ppermute x7, starting transfers between devices, along(): lax.ppermute(a, LINE, [(index[(i + by) % n], index[i]) for i in range(n)])  14 us
    all_to_all x1, waiting for transfers between devices, on_device(): spread = lax.all_to_all(blocks, BLK, 0, 0, tiled=True)  11.7 us
    pallas_call x2, Pallas kernels, product(): pl.pallas_call(functools.partial(product_kernel, groups, len(near)), out_...  11 us
    all_to_all x1, starting transfers between devices, on_device(): spread = lax.all_to_all(blocks, BLK, 0, 0, tiled=True)  10.1 us
    unnamed x25, local copies, waits for them, and re-layouts  6.29 us
  transfers between devices with their start and end apart: 25, of which 12 were waited for; matrix products, arithmetic and copies ran while one was open for 5% of the time, Pallas kernels for 4%

profile of v4, /device:TPU:1, one launch (start us, length us, event | category | flops | bytes accessed | tf_op | source)
XLA Modules:
  0.0 165.6 jit_solution(13258897139682595979)
XLA Ops:
  3.5 10.1 %all-to-all-start = ((bf16[32,32,256]{2,1,0:T(8,128)(2,1)}), bf16[32,32,256]{2,1,0:T(8,128)(2,1)S(1)}, u32[]{:S(2)}, u32[]{:S(2)}) async-start(bf16[32,32,256]{2,1,0:T(8,128)(2,1)} %get-tuple-element.20), calls=%async_computation | async-start | bytes 1048576 | tf_op jit(solution)/shard_map/all_to_all | solution.py:180
  13.8 2.7 %collective-permute-start.2 = (bf16[2,128,256]{2,1,0:T(8,128)(2,1)S(1)}, bf16[2,128,256]{2,1,0:T(8,128)(2,1)S(1)}, u32[]{:S(2)}, u32[]{:S(2)}) collective-permute-start(bf16[2,128,256]{2,1,0:T(8,128)(2,1)S(1)} %get-tuple-element.45), channel_id=1, source_target_pairs={{16,0},{32,16},{48,32},{0,48},{17,1},{33,17},{49,33},{1,49},{18,2}... | collective-permute-start | bytes 393224 | tf_op jit(solution)/shard_map/ppermute | solution.py:26
  18.3 11.7 %all-to-all-done.spread = bf16[32,32,256]{2,1,0:T(8,128)(2,1)S(1)} async-done(((bf16[32,32,256]{2,1,0:T(8,128)(2,1)}), bf16[32,32,256]{2,1,0:T(8,128)(2,1)S(1)}, u32[]{:S(2)}, u32[]{:S(2)}) %all-to-all-start) | async-done | bytes 524320 | tf_op jit(solution)/shard_map/all_to_all | solution.py:180
  32.8 4.2 %all-to-all-start.1 = ((bf16[4,2,32,1024]{3,2,1,0:T(8,128)(2,1)}), bf16[4,2,32,1024]{3,2,1,0:T(8,128)(2,1)S(1)}, u32[]{:S(2)}, u32[]{:S(2)}) async-start(bf16[4,2,32,1024]{3,2,1,0:T(8,128)(2,1)} %pick.1), calls=%async_computation.1 | async-start | bytes 1048576 | tf_op jit(solution)/shard_map/all_to_all | solution.py:198
  37.0 4.3 %collective-permute-start.5 = (bf16[4,2,128,256]{3,2,1,0:T(8,128)(2,1)S(1)}, bf16[4,2,128,256]{3,2,1,0:T(8,128)(2,1)S(1)}, u32[]{:S(2)}, u32[]{:S(2)}) collective-permute-start(bf16[4,2,128,256]{3,2,1,0:T(8,128)(2,1)S(1)} %pad_maximum_fusion.2.refs_4_), channel_id=1, source_target_pairs={{1,0},{0,1},{3,2},{2,3},{5,4},{4,5},{7,6},{6,7},{9,8},{8,9},{11,10... | collective-permute-start | bytes 1572872 | tf_op jit(solution)/shard_map/ppermute | solution.py:26
  41.3 5.3 %all-to-all-done.1 = bf16[4,2,32,1024]{3,2,1,0:T(8,128)(2,1)S(1)} async-done(((bf16[4,2,32,1024]{3,2,1,0:T(8,128)(2,1)}), bf16[4,2,32,1024]{3,2,1,0:T(8,128)(2,1)S(1)}, u32[]{:S(2)}, u32[]{:S(2)}) %all-to-all-start.1) | async-done | bytes 524320 | tf_op jit(solution)/shard_map/all_to_all | solution.py:198
  47.8 2.7 %collective-permute-start = (bf16[128,1024]{1,0:T(8,128)(2,1)}, bf16[128,1024]{1,0:T(8,128)(2,1)S(1)}, u32[]{:S(2)}, u32[]{:S(2)}) collective-permute-start(bf16[128,1024]{1,0:T(8,128)(2,1)} %bitcast.22), channel_id=1, source_target_pairs={{64,0},{128,64},{192,128},{1,192},{65,1},{129,65},{193,129},{0,193... | collective-permute-start | bytes 786440 | tf_op jit(solution)/shard_map/ppermute | solution.py:32
  52.6 12.5 %collective-permute-done.5 = bf16[4,2,128,256]{3,2,1,0:T(8,128)(2,1)S(1)} collective-permute-done((bf16[4,2,128,256]{3,2,1,0:T(8,128)(2,1)S(1)}, bf16[4,2,128,256]{3,2,1,0:T(8,128)(2,1)S(1)}, u32[]{:S(2)}, u32[]{:S(2)}) %collective-permute-start.5) | collective-permute-done | bytes 524320 | tf_op jit(solution)/shard_map/ppermute | solution.py:26
  66.6 4.4 %all-to-all-start.2 = ((bf16[4,4,2,128,256]{4,3,2,1,0:T(8,128)(2,1)}), bf16[4,4,2,128,256]{4,3,2,1,0:T(8,128)(2,1)}, u32[]{:S(2)}, u32[]{:S(2)}) async-start(bf16[4,4,2,128,256]{4,3,2,1,0:T(8,128)(2,1)} %broadcast_in_dim.23), calls=%async_computation.2 | async-start | bytes 4194304 | tf_op jit(solution)/shard_map/all_to_all | solution.py:194
  73.2 2.4 %collective-permute-start.7 = (bf16[128,1024]{1,0:T(8,128)(2,1)}, bf16[128,1024]{1,0:T(8,128)(2,1)S(1)}, u32[]{:S(2)}, u32[]{:S(2)}) collective-permute-start(bf16[128,1024]{1,0:T(8,128)(2,1)} %bitcast.96), channel_id=1, source_target_pairs={{129,0},{193,64},{0,128},{64,192},{128,1},{192,65},{1,129},{65,193... | collective-permute-start | bytes 786440 | tf_op jit(solution)/shard_map/ppermute | solution.py:32
  77.0 8.3 %collective-permute-done.6 = bf16[128,1024]{1,0:T(8,128)(2,1)S(1)} collective-permute-done((bf16[128,1024]{1,0:T(8,128)(2,1)}, bf16[128,1024]{1,0:T(8,128)(2,1)S(1)}, u32[]{:S(2)}, u32[]{:S(2)}) %collective-permute-start.6) | collective-permute-done | bytes 262176 | tf_op jit(solution)/shard_map/ppermute | solution.py:32
  86.7 7.3 %collective-permute-start.8 = (bf16[5,4,32,1024]{3,2,1,0:T(8,128)(2,1)}, bf16[5,4,32,1024]{3,2,1,0:T(8,128)(2,1)}, u32[]{:S(2)}, u32[]{:S(2)}) collective-permute-start(bf16[5,4,32,1024]{3,2,1,0:T(8,128)(2,1)} %constant_dynamic-update-slice_fusion.refs_0_), channel_id=1, source_target_pairs={{8,0},{0,8},{9,1},{1,9},{10,2},{2,10},{11,3},{3,11},{12,4},{4,12},... | collective-permute-start | bytes 3932168 | tf_op jit(solution)/shard_map/ppermute | solution.py:26
  94.1 3.3 %collective-permute-start.10 = (bf16[128,1024]{1,0:T(8,128)(2,1)S(1)}, bf16[128,1024]{1,0:T(8,128)(2,1)S(1)}, u32[]{:S(2)}, u32[]{:S(2)}) collective-permute-start(bf16[128,1024]{1,0:T(8,128)(2,1)S(1)} %bitcast.94), channel_id=1, source_target_pairs={{65,0},{129,64},{193,128},{0,192},{64,1},{128,65},{192,129},{1,193... | collective-permute-start | bytes 786440 | tf_op jit(solution)/shard_map/ppermute | solution.py:32
  97.4 9.6 %collective-permute-done.13.refs_7_ = bf16[4,2,128,256]{3,2,1,0:T(8,128)(2,1)S(1)} collective-permute-done((bf16[4,2,128,256]{3,2,1,0:T(8,128)(2,1)S(1)}, bf16[4,2,128,256]{3,2,1,0:T(8,128)(2,1)S(1)}, u32[]{:S(2)}, u32[]{:S(2)}) %collective-permute-start.13) | collective-permute-done | bytes 524320 | tf_op jit(solution)/shard_map/ppermute | solution.py:26
  107.8 5.6 %collective-permute-start.14 = (bf16[128,1024]{1,0:T(8,128)(2,1)S(1)}, bf16[128,1024]{1,0:T(8,128)(2,1)S(1)}, u32[]{:S(2)}, u32[]{:S(2)}) collective-permute-start(bf16[128,1024]{1,0:T(8,128)(2,1)S(1)} %bitcast.93), channel_id=1, source_target_pairs={{1,0},{65,64},{129,128},{193,192},{0,1},{64,65},{128,129},{192,193... | collective-permute-start | bytes 786440 | tf_op jit(solution)/shard_map/ppermute | solution.py:32
  114.1 3.1 %collective-permute-done.10 = bf16[128,1024]{1,0:T(8,128)(2,1)S(1)} collective-permute-done((bf16[128,1024]{1,0:T(8,128)(2,1)S(1)}, bf16[128,1024]{1,0:T(8,128)(2,1)S(1)}, u32[]{:S(2)}, u32[]{:S(2)}) %collective-permute-start.10) | collective-permute-done | bytes 262176 | tf_op jit(solution)/shard_map/ppermute | solution.py:32
  117.2 8.5 %collective-permute-done.14 = bf16[128,1024]{1,0:T(8,128)(2,1)S(1)} collective-permute-done((bf16[128,1024]{1,0:T(8,128)(2,1)S(1)}, bf16[128,1024]{1,0:T(8,128)(2,1)S(1)}, u32[]{:S(2)}, u32[]{:S(2)}) %collective-permute-start.14) | collective-permute-done | bytes 262176 | tf_op jit(solution)/shard_map/ppermute | solution.py:32
  130.6 5.5 %product.2 = (f32[512,256]{1,0:T(8,128)S(1)}, f32[2,272,256]{2,1,0:T(8,128)S(1)}, f32[2,272,256]{2,1,0:T(8,128)S(1)}, f32[2,272,256]{2,1,0:T(8,128)S(1)}) custom-call(s32[20]{0:T(128)S(1)} %stack.126.at, bf16[5,4,32,1024]{3,2,1,0:T(8,128)(2,1)} %constant_dynamic-update-slice_fusion.refs_0_, bf16[5,4,32,1024]{3,2,1,0:T(8,128)(2,1)} %collective-permute-done.8.refs_1_, ...), custom_call_target="tpu_custom_call" | custom-call | flops 2147483648 | bytes 8388608 | tf_op jit(solution)/shard_map/product/pallas_call | solution.py:144
  136.3 2.6 %collective-permute-start.17 = (f16[2,272,256]{2,1,0:T(8,128)(2,1)S(1)}, f16[2,272,256]{2,1,0:T(8,128)(2,1)S(1)}, u32[]{:S(2)}, u32[]{:S(2)}) collective-permute-start(f16[2,272,256]{2,1,0:T(8,128)(2,1)S(1)} %convert_element_type.61), channel_id=1, source_target_pairs={{48,0},{0,16},{16,32},{32,48},{49,1},{1,17},{17,33},{33,49},{50,2}... | collective-permute-start | bytes 835592 | tf_op jit(solution)/shard_map/ppermute | solution.py:26
  139.2 5.5 %product.3 = (f32[512,256]{1,0:T(8,128)S(1)}, f32[2,272,256]{2,1,0:T(8,128)S(1)}, f32[2,272,256]{2,1,0:T(8,128)S(1)}, f32[2,272,256]{2,1,0:T(8,128)S(1)}) custom-call(s32[20]{0:T(128)S(1)} %stack.126.at, bf16[5,4,32,1024]{3,2,1,0:T(8,128)(2,1)} %constant_dynamic-update-slice_fusion.refs_0_, bf16[5,4,32,1024]{3,2,1,0:T(8,128)(2,1)} %collective-permute-done.8.refs_1_, ...), custom_call_target="tpu_custom_call" | custom-call | flops 2147483648 | bytes 8388608 | tf_op jit(solution)/shard_map/product/pallas_call | solution.py:144
  146.8 2.7 %collective-permute-start.21 = (f16[2,272,256]{2,1,0:T(8,128)(2,1)S(1)}, f16[2,272,256]{2,1,0:T(8,128)(2,1)S(1)}, u32[]{:S(2)}, u32[]{:S(2)}) collective-permute-start(f16[2,272,256]{2,1,0:T(8,128)(2,1)S(1)} %convert_element_type.73), channel_id=1, source_target_pairs={{16,0},{32,16},{48,32},{0,48},{17,1},{33,17},{49,33},{1,49},{18,2}... | collective-permute-start | bytes 835592 | tf_op jit(solution)/shard_map/ppermute | solution.py:26
  149.5 2.8 %collective-permute-done.17 = f16[2,272,256]{2,1,0:T(8,128)(2,1)S(1)} collective-permute-done((f16[2,272,256]{2,1,0:T(8,128)(2,1)S(1)}, f16[2,272,256]{2,1,0:T(8,128)(2,1)S(1)}, u32[]{:S(2)}, u32[]{:S(2)}) %collective-permute-start.17) | collective-permute-done | bytes 278560 | tf_op jit(solution)/shard_map/ppermute | solution.py:26
  152.4 5.3 %collective-permute-done.19 = f16[2,272,256]{2,1,0:T(8,128)(2,1)S(1)} collective-permute-done((f16[2,272,256]{2,1,0:T(8,128)(2,1)S(1)}, f16[2,272,256]{2,1,0:T(8,128)(2,1)S(1)}, u32[]{:S(2)}, u32[]{:S(2)}) %collective-permute-start.19) | collective-permute-done | bytes 278560 | tf_op jit(solution)/shard_map/ppermute | solution.py:26
  157.7 6.2 %collective-permute-done.20 = f16[2,272,256]{2,1,0:T(8,128)(2,1)S(1)} collective-permute-done((f16[2,272,256]{2,1,0:T(8,128)(2,1)S(1)}, f16[2,272,256]{2,1,0:T(8,128)(2,1)S(1)}, u32[]{:S(2)}, u32[]{:S(2)}) %collective-permute-start.20) | collective-permute-done | bytes 278560 | tf_op jit(solution)/shard_map/ppermute | solution.py:26
  (85 shorter events, 28.5 us)
Async XLA Ops:
  3.5 26.6 %all-to-all-start = ((bf16[32,32,256]{2,1,0:T(8,128)(2,1)}), bf16[32,32,256]{2,1,0:T(8,128)(2,1)S(1)}, u32[]{:S(2)}, u32[]{:S(2)}) async-start(bf16[32,32,256]{2,1,0:T(8,128)(2,1)} %get-tuple-element.20), calls=%async_computation | async-start | bytes 1048576 | tf_op jit(solution)/shard_map/all_to_all | solution.py:180
  13.8 23.1 %collective-permute-start.2 = (bf16[2,128,256]{2,1,0:T(8,128)(2,1)S(1)}, bf16[2,128,256]{2,1,0:T(8,128)(2,1)S(1)}, u32[]{:S(2)}, u32[]{:S(2)}) collective-permute-start(bf16[2,128,256]{2,1,0:T(8,128)(2,1)S(1)} %get-tuple-element.45), channel_id=1, source_target_pairs={{16,0},{32,16},{48,32},{0,48},{17,1},{33,17},{49,33},{1,49},{18,2}... | collective-permute-start | bytes 393224 | tf_op jit(solution)/shard_map/ppermute | solution.py:26
  16.5 20.5 %collective-permute-start.3 = (bf16[2,128,256]{2,1,0:T(8,128)(2,1)S(1)}, bf16[2,128,256]{2,1,0:T(8,128)(2,1)S(1)}, u32[]{:S(2)}, u32[]{:S(2)}) collective-permute-start(bf16[2,128,256]{2,1,0:T(8,128)(2,1)S(1)} %get-tuple-element.44), channel_id=1, source_target_pairs={{32,0},{48,16},{0,32},{16,48},{33,1},{49,17},{1,33},{17,49},{34,2}... | collective-permute-start | bytes 393224 | tf_op jit(solution)/shard_map/ppermute | solution.py:26
  17.1 19.9 %collective-permute-start.4 = (bf16[2,128,256]{2,1,0:T(8,128)(2,1)S(1)}, bf16[2,128,256]{2,1,0:T(8,128)(2,1)S(1)}, u32[]{:S(2)}, u32[]{:S(2)}) collective-permute-start(bf16[2,128,256]{2,1,0:T(8,128)(2,1)S(1)} %get-tuple-element.43), channel_id=1, source_target_pairs={{48,0},{0,16},{16,32},{32,48},{49,1},{1,17},{17,33},{33,49},{50,2}... | collective-permute-start | bytes 393224 | tf_op jit(solution)/shard_map/ppermute | solution.py:26
  32.8 13.9 %all-to-all-start.1 = ((bf16[4,2,32,1024]{3,2,1,0:T(8,128)(2,1)}), bf16[4,2,32,1024]{3,2,1,0:T(8,128)(2,1)S(1)}, u32[]{:S(2)}, u32[]{:S(2)}) async-start(bf16[4,2,32,1024]{3,2,1,0:T(8,128)(2,1)} %pick.1), calls=%async_computation.1 | async-start | bytes 1048576 | tf_op jit(solution)/shard_map/all_to_all | solution.py:198
  37.0 28.0 %collective-permute-start.5 = (bf16[4,2,128,256]{3,2,1,0:T(8,128)(2,1)S(1)}, bf16[4,2,128,256]{3,2,1,0:T(8,128)(2,1)S(1)}, u32[]{:S(2)}, u32[]{:S(2)}) collective-permute-start(bf16[4,2,128,256]{3,2,1,0:T(8,128)(2,1)S(1)} %pad_maximum_fusion.2.refs_4_), channel_id=1, source_target_pairs={{1,0},{0,1},{3,2},{2,3},{5,4},{4,5},{7,6},{6,7},{9,8},{8,9},{11,10... | collective-permute-start | bytes 1572872 | tf_op jit(solution)/shard_map/ppermute | solution.py:26
  47.8 24.1 %collective-permute-start = (bf16[128,1024]{1,0:T(8,128)(2,1)}, bf16[128,1024]{1,0:T(8,128)(2,1)S(1)}, u32[]{:S(2)}, u32[]{:S(2)}) collective-permute-start(bf16[128,1024]{1,0:T(8,128)(2,1)} %bitcast.22), channel_id=1, source_target_pairs={{64,0},{128,64},{192,128},{1,192},{65,1},{129,65},{193,129},{0,193... | collective-permute-start | bytes 786440 | tf_op jit(solution)/shard_map/ppermute | solution.py:32
  50.5 22.7 %collective-permute-start.1 = (bf16[128,1024]{1,0:T(8,128)(2,1)}, bf16[128,1024]{1,0:T(8,128)(2,1)S(1)}, u32[]{:S(2)}, u32[]{:S(2)}) collective-permute-start(bf16[128,1024]{1,0:T(8,128)(2,1)} %bitcast.24), channel_id=1, source_target_pairs={{193,0},{0,64},{64,128},{128,192},{192,1},{1,65},{65,129},{129,193... | collective-permute-start | bytes 786440 | tf_op jit(solution)/shard_map/ppermute | solution.py:32
  50.5 43.6 %collective-permute-start.11 = (bf16[4,2,128,256]{3,2,1,0:T(8,128)(2,1)S(1)}, bf16[4,2,128,256]{3,2,1,0:T(8,128)(2,1)S(1)}, u32[]{:S(2)}, u32[]{:S(2)}) collective-permute-start(bf16[4,2,128,256]{3,2,1,0:T(8,128)(2,1)S(1)} %pad_maximum_fusion.2.refs_4_), channel_id=1, source_target_pairs={{2,0},{4,2},{6,4},{0,6},{3,1},{5,3},{7,5},{1,7},{10,8},{12,10},{14... | collective-permute-start | bytes 1572872 | tf_op jit(solution)/shard_map/ppermute | solution.py:26
  51.4 46.0 %collective-permute-start.12 = (bf16[4,2,128,256]{3,2,1,0:T(8,128)(2,1)S(1)}, bf16[4,2,128,256]{3,2,1,0:T(8,128)(2,1)S(1)}, u32[]{:S(2)}, u32[]{:S(2)}) collective-permute-start(bf16[4,2,128,256]{3,2,1,0:T(8,128)(2,1)S(1)} %pad_maximum_fusion.2.refs_4_), channel_id=1, source_target_pairs={{4,0},{6,2},{0,4},{2,6},{5,1},{7,3},{1,5},{3,7},{12,8},{14,10},{8,... | collective-permute-start | bytes 1572872 | tf_op jit(solution)/shard_map/ppermute | solution.py:26
  66.6 61.1 %all-to-all-start.2 = ((bf16[4,4,2,128,256]{4,3,2,1,0:T(8,128)(2,1)}), bf16[4,4,2,128,256]{4,3,2,1,0:T(8,128)(2,1)}, u32[]{:S(2)}, u32[]{:S(2)}) async-start(bf16[4,4,2,128,256]{4,3,2,1,0:T(8,128)(2,1)} %broadcast_in_dim.23), calls=%async_computation.2 | async-start | bytes 4194304 | tf_op jit(solution)/shard_map/all_to_all | solution.py:194
  71.1 14.2 %collective-permute-start.6 = (bf16[128,1024]{1,0:T(8,128)(2,1)}, bf16[128,1024]{1,0:T(8,128)(2,1)S(1)}, u32[]{:S(2)}, u32[]{:S(2)}) collective-permute-start(bf16[128,1024]{1,0:T(8,128)(2,1)} %bitcast.97), channel_id=1, source_target_pairs={{128,0},{192,64},{1,128},{65,192},{129,1},{193,65},{0,129},{64,193... | collective-permute-start | bytes 786440 | tf_op jit(solution)/shard_map/ppermute | solution.py:32
  71.9 35.1 %collective-permute-start.13 = (bf16[4,2,128,256]{3,2,1,0:T(8,128)(2,1)S(1)}, bf16[4,2,128,256]{3,2,1,0:T(8,128)(2,1)S(1)}, u32[]{:S(2)}, u32[]{:S(2)}) collective-permute-start(bf16[4,2,128,256]{3,2,1,0:T(8,128)(2,1)S(1)} %pad_maximum_fusion.2.refs_4_), channel_id=1, source_target_pairs={{6,0},{0,2},{2,4},{4,6},{7,1},{1,3},{3,5},{5,7},{14,8},{8,10},{10,... | collective-permute-start | bytes 1572872 | tf_op jit(solution)/shard_map/ppermute | solution.py:26
  73.2 12.8 %collective-permute-start.7 = (bf16[128,1024]{1,0:T(8,128)(2,1)}, bf16[128,1024]{1,0:T(8,128)(2,1)S(1)}, u32[]{:S(2)}, u32[]{:S(2)}) collective-permute-start(bf16[128,1024]{1,0:T(8,128)(2,1)} %bitcast.96), channel_id=1, source_target_pairs={{129,0},{193,64},{0,128},{64,192},{128,1},{192,65},{1,129},{65,193... | collective-permute-start | bytes 786440 | tf_op jit(solution)/shard_map/ppermute | solution.py:32
  86.7 42.8 %collective-permute-start.8 = (bf16[5,4,32,1024]{3,2,1,0:T(8,128)(2,1)}, bf16[5,4,32,1024]{3,2,1,0:T(8,128)(2,1)}, u32[]{:S(2)}, u32[]{:S(2)}) collective-permute-start(bf16[5,4,32,1024]{3,2,1,0:T(8,128)(2,1)} %constant_dynamic-update-slice_fusion.refs_0_), channel_id=1, source_target_pairs={{8,0},{0,8},{9,1},{1,9},{10,2},{2,10},{11,3},{3,11},{12,4},{4,12},... | collective-permute-start | bytes 3932168 | tf_op jit(solution)/shard_map/ppermute | solution.py:26
  94.1 20.1 %collective-permute-start.9 = (bf16[128,1024]{1,0:T(8,128)(2,1)S(1)}, bf16[128,1024]{1,0:T(8,128)(2,1)S(1)}, u32[]{:S(2)}, u32[]{:S(2)}) collective-permute-start(bf16[128,1024]{1,0:T(8,128)(2,1)S(1)} %bitcast.95), channel_id=1, source_target_pairs={{192,0},{1,64},{65,128},{129,192},{193,1},{0,65},{64,129},{128,193... | collective-permute-start | bytes 786440 | tf_op jit(solution)/shard_map/ppermute | solution.py:32
  94.1 23.1 %collective-permute-start.10 = (bf16[128,1024]{1,0:T(8,128)(2,1)S(1)}, bf16[128,1024]{1,0:T(8,128)(2,1)S(1)}, u32[]{:S(2)}, u32[]{:S(2)}) collective-permute-start(bf16[128,1024]{1,0:T(8,128)(2,1)S(1)} %bitcast.94), channel_id=1, source_target_pairs={{65,0},{129,64},{193,128},{0,192},{64,1},{128,65},{192,129},{1,193... | collective-permute-start | bytes 786440 | tf_op jit(solution)/shard_map/ppermute | solution.py:32
  107.8 18.0 %collective-permute-start.14 = (bf16[128,1024]{1,0:T(8,128)(2,1)S(1)}, bf16[128,1024]{1,0:T(8,128)(2,1)S(1)}, u32[]{:S(2)}, u32[]{:S(2)}) collective-permute-start(bf16[128,1024]{1,0:T(8,128)(2,1)S(1)} %bitcast.93), channel_id=1, source_target_pairs={{1,0},{65,64},{129,128},{193,192},{0,1},{64,65},{128,129},{192,193... | collective-permute-start | bytes 786440 | tf_op jit(solution)/shard_map/ppermute | solution.py:32
  136.2 10.6 %collective-permute-start.16 = (f16[2,272,256]{2,1,0:T(8,128)(2,1)S(1)}, f16[2,272,256]{2,1,0:T(8,128)(2,1)S(1)}, u32[]{:S(2)}, u32[]{:S(2)}) collective-permute-start(f16[2,272,256]{2,1,0:T(8,128)(2,1)S(1)} %convert_element_type.58), channel_id=1, source_target_pairs={{32,0},{48,16},{0,32},{16,48},{33,1},{49,17},{1,33},{17,49},{34,2}... | collective-permute-start | bytes 835592 | tf_op jit(solution)/shard_map/ppermute | solution.py:26
  136.3 16.0 %collective-permute-start.17 = (f16[2,272,256]{2,1,0:T(8,128)(2,1)S(1)}, f16[2,272,256]{2,1,0:T(8,128)(2,1)S(1)}, u32[]{:S(2)}, u32[]{:S(2)}) collective-permute-start(f16[2,272,256]{2,1,0:T(8,128)(2,1)S(1)} %convert_element_type.61), channel_id=1, source_target_pairs={{48,0},{0,16},{16,32},{32,48},{49,1},{1,17},{17,33},{33,49},{50,2}... | collective-permute-start | bytes 835592 | tf_op jit(solution)/shard_map/ppermute | solution.py:26
  138.9 13.4 %collective-permute-start.18 = (f16[2,272,256]{2,1,0:T(8,128)(2,1)S(1)}, f16[2,272,256]{2,1,0:T(8,128)(2,1)S(1)}, u32[]{:S(2)}, u32[]{:S(2)}) collective-permute-start(f16[2,272,256]{2,1,0:T(8,128)(2,1)S(1)} %convert_element_type.64), channel_id=1, source_target_pairs={{16,0},{32,16},{48,32},{0,48},{17,1},{33,17},{49,33},{1,49},{18,2}... | collective-permute-start | bytes 835592 | tf_op jit(solution)/shard_map/ppermute | solution.py:26
  144.8 12.9 %collective-permute-start.19 = (f16[2,272,256]{2,1,0:T(8,128)(2,1)S(1)}, f16[2,272,256]{2,1,0:T(8,128)(2,1)S(1)}, u32[]{:S(2)}, u32[]{:S(2)}) collective-permute-start(f16[2,272,256]{2,1,0:T(8,128)(2,1)S(1)} %convert_element_type.67), channel_id=1, source_target_pairs={{32,0},{48,16},{0,32},{16,48},{33,1},{49,17},{1,33},{17,49},{34,2}... | collective-permute-start | bytes 835592 | tf_op jit(solution)/shard_map/ppermute | solution.py:26
  146.6 17.3 %collective-permute-start.20 = (f16[2,272,256]{2,1,0:T(8,128)(2,1)S(1)}, f16[2,272,256]{2,1,0:T(8,128)(2,1)S(1)}, u32[]{:S(2)}, u32[]{:S(2)}) collective-permute-start(f16[2,272,256]{2,1,0:T(8,128)(2,1)S(1)} %convert_element_type.70), channel_id=1, source_target_pairs={{48,0},{0,16},{16,32},{32,48},{49,1},{1,17},{17,33},{33,49},{50,2}... | collective-permute-start | bytes 835592 | tf_op jit(solution)/shard_map/ppermute | solution.py:26
  146.8 17.2 %collective-permute-start.21 = (f16[2,272,256]{2,1,0:T(8,128)(2,1)S(1)}, f16[2,272,256]{2,1,0:T(8,128)(2,1)S(1)}, u32[]{:S(2)}, u32[]{:S(2)}) collective-permute-start(f16[2,272,256]{2,1,0:T(8,128)(2,1)S(1)} %convert_element_type.73), channel_id=1, source_target_pairs={{16,0},{32,16},{48,32},{0,48},{17,1},{33,17},{49,33},{1,49},{18,2}... | collective-permute-start | bytes 835592 | tf_op jit(solution)/shard_map/ppermute | solution.py:26
  (8 other events, 78.9 us)
